TPU v7x, 256 devices: a whole 4x4x8 slice. The times are simulated.
256 devices in a mesh: wide: 16 (over z_hi, y), col: 16 (over x, z_lo, core).
Axes of the slice: x: 4, y: 4, z: 8 (z_hi: 4, z_lo: 2; z = z_hi * 2 + z_lo), core: 2. Of those that a mesh axis runs over, the one named last changes fastest.
Arguments:
- object_field: float32 [2, 8192, 8192], P(None, 'wide', 'col'), may hold values from -6 to 6
- probe_modes: float32 [2, 4, 128, 128], replicated, may hold values from -3 to 3
- amplitude: bfloat16 [16, 16, 32, 128, 128], P('wide', 'col'), may hold values from 0 to 4
- positions: int32 [16, 16, 32, 2], P('wide', 'col'), may hold values from 0 to 511
- slot_counts: int32 [16, 16], P('wide', 'col'), may hold values from 4 to 32, as said below
Outputs:
- new_object: float32 [2, 8192, 8192], P(None, 'wide', 'col')
- probe_direction: float32 [2, 4, 128, 128], replicated
Inputs may be any that keep to these rules, and one draw needn't show every extreme that they name: `positions`: offsets lie inside the device's own tile. The live slots of a device are its first slot_counts[w, c] slots; at least one device has all 32 slots live.
All inputs are finite; a program needn't handle non-finite values.
Results may differ from a plain program's by a relative error of at most 0.0017.
The roundings to bfloat16 on the way count: a program that leaves them out, or rounds other values in their place, can miss the bound.
Values sent between devices are 32-bit elements; how exact they have to be, the bound alone decides.
A program may use at most 128 MiB of HBM per device.

v0:
```python
import math

import jax
import jax.numpy as jnp
from jax import lax
from jax.sharding import PartitionSpec as P


def shifted(value, axis, steps):
    count = lax.axis_size(axis)
    initial, last = (max(0, -steps), min(count, count - steps))
    return lax.ppermute(value, axis, [(source, source + steps) for source in range(initial, last)])


def dft_tables(length, sign_value):
    indices = jnp.arange(length, dtype=jnp.int32)
    product = indices[:, None] * indices[None, :] % length
    angles = product.astype(jnp.float32) * (2.0 * math.pi / length)
    factor = 1.0 / math.sqrt(length)
    cosine = jnp.cos(angles) * factor
    sine = -sign_value * jnp.sin(angles) * factor
    left_table = jnp.stack([jnp.stack([cosine, -sine], 1), jnp.stack([sine, cosine], 1)], 0)
    right_table = jnp.transpose(left_table, (2, 3, 0, 1))
    return (left_table.astype(jnp.bfloat16), right_table.astype(jnp.bfloat16))


def patch_terms(patches, probe_modes, block_amps, valid, tables):
    fwd_left, fwd_right, inv_left, inv_right = tables
    probe_re = probe_modes[0][None]
    probe_im = probe_modes[1][None]
    patch_re = patches[:, 0][:, None]
    patch_im = patches[:, 1][:, None]
    exit_re = probe_re * patch_re - probe_im * patch_im
    exit_im = probe_re * patch_im + probe_im * patch_re
    exit_wave = jnp.stack([exit_re, exit_im], 2).astype(jnp.bfloat16)
    half = jnp.einsum(
        "cjdk,bmdkl->bmcjl", fwd_left, exit_wave, preferred_element_type=jnp.float32
    ).astype(jnp.bfloat16)
    farfield = jnp.einsum("bmdjk,dkcl->bmcjl", half, fwd_right, preferred_element_type=jnp.float32)
    intensity = jnp.sum(farfield * farfield, axis=(1, 2))
    factor = (block_amps.astype(jnp.float32) / jnp.sqrt(jnp.maximum(intensity, 1.0)) - 1.0) * valid[
        :, None, None
    ]
    residual_wave = (farfield * factor[:, None, None]).astype(jnp.bfloat16)
    half_back = jnp.einsum(
        "cjdk,bmdkl->bmcjl", inv_left, residual_wave, preferred_element_type=jnp.float32
    ).astype(jnp.bfloat16)
    update = jnp.einsum(
        "bmdjk,dkcl->bmcjl", half_back, inv_right, preferred_element_type=jnp.float32
    )
    update_re = update[:, :, 0]
    update_im = update[:, :, 1]
    grad_re = jnp.sum(probe_re * update_re + probe_im * update_im, axis=1)
    grad_im = jnp.sum(probe_re * update_im - probe_im * update_re, axis=1)
    patch_grad = jnp.stack([grad_re, grad_im], 1)
    term_re = jnp.sum(patch_re * update_re + patch_im * update_im, axis=0)
    term_im = jnp.sum(patch_re * update_im - patch_im * update_re, axis=0)
    probe_term = jnp.stack([term_re, term_im], 0)
    illum_term = jnp.sum(
        valid[:, None, None] * (patches[:, 0] * patches[:, 0] + patches[:, 1] * patches[:, 1]),
        axis=0,
    )
    return (patch_grad, probe_term, illum_term)


def local(object_field, probe_modes, amplitude, positions, slot_counts):
    tile_size = object_field.shape[1]
    patch_size = probe_modes.shape[2]
    slot_count = positions.shape[2]
    block_size = 8
    fwd_left, fwd_right = dft_tables(patch_size, 1.0)
    inv_left, inv_right = dft_tables(patch_size, -1.0)
    tables = (fwd_left, fwd_right, inv_left, inv_right)
    right_part = shifted(object_field[:, :, :patch_size], "col", -1)
    widened = jnp.concatenate([object_field, right_part], 2)
    lower_part = shifted(widened[:, :patch_size, :], "wide", -1)
    extended = jnp.concatenate([widened, lower_part], 1)
    live_slots = slot_counts[0, 0]
    local_positions = positions.reshape(slot_count, 2)
    local_amps = amplitude.reshape(slot_count, patch_size, patch_size)
    power = jnp.sum(probe_modes * probe_modes, axis=(0, 1))

    def run_block(block_index, totals):
        grad_ext, weight_ext, probe_total, illum_total = totals
        first_slot = block_index * block_size
        chosen = lax.dynamic_slice_in_dim(local_positions, first_slot, block_size, 0)
        block_amps = lax.dynamic_slice_in_dim(local_amps, first_slot, block_size, 0)
        valid = (first_slot + jnp.arange(block_size, dtype=jnp.int32) < live_slots).astype(
            jnp.float32
        )
        patches = jnp.stack(
            [
                lax.dynamic_slice(
                    extended, (0, chosen[slot, 0], chosen[slot, 1]), (2, patch_size, patch_size)
                )
                for slot in range(block_size)
            ],
            0,
        )
        patch_grad, probe_term, illum_term = patch_terms(
            patches, probe_modes, block_amps, valid, tables
        )
        for slot in range(block_size):
            row_at = chosen[slot, 0]
            col_at = chosen[slot, 1]
            window = lax.dynamic_slice(grad_ext, (0, row_at, col_at), (2, patch_size, patch_size))
            grad_ext = lax.dynamic_update_slice(
                grad_ext, window + patch_grad[slot], (0, row_at, col_at)
            )
            spot = lax.dynamic_slice(weight_ext, (row_at, col_at), (patch_size, patch_size))
            weight_ext = lax.dynamic_update_slice(
                weight_ext, spot + valid[slot] * power, (row_at, col_at)
            )
        return (grad_ext, weight_ext, probe_total + probe_term, illum_total + illum_term)

    initial = (
        jnp.zeros(extended.shape, jnp.float32),
        jnp.zeros(extended.shape[1:], jnp.float32),
        jnp.zeros(probe_modes.shape, jnp.float32),
        jnp.zeros((patch_size, patch_size), jnp.float32),
    )
    block_total = slot_count // block_size
    grad_ext, weight_ext, probe_total, illum_total = lax.fori_loop(
        0, block_total, run_block, initial
    )
    payload = (grad_ext[:, tile_size:, :], weight_ext[tile_size:, :])
    returned = shifted((payload[0], payload[1]), "wide", 1)
    grad_ext = grad_ext.at[:, :patch_size, :].add(returned[0])
    weight_ext = weight_ext.at[:patch_size, :].add(returned[1])
    payload = (grad_ext[:, :tile_size, tile_size:], weight_ext[:tile_size, tile_size:])
    returned = shifted((payload[0], payload[1]), "col", 1)
    object_grad = grad_ext[:, :tile_size, :tile_size].at[:, :, :patch_size].add(returned[0])
    object_weight = weight_ext[:tile_size, :tile_size].at[:, :patch_size].add(returned[1])
    new_object = object_field + object_grad / (object_weight + 1.0)[None]
    summed_grad, summed_illum = lax.psum((probe_total, illum_total), ("wide", "col"))
    probe_direction = summed_grad / jnp.sqrt(summed_illum + 1.0)[None, None]
    return (new_object, probe_direction)


def solution(mesh):
    placed = (
        P(None, "wide", "col"),
        P(),
        P("wide", "col", None, None, None),
        P("wide", "col", None, None),
        P("wide", "col"),
    )
    return jax.shard_map(
        local, mesh=mesh, in_specs=placed, out_specs=(P(None, "wide", "col"), P()), check_vma=False
    )
```

profile of v0, /device:TPU:1, one launch (start us, length us, event | category | flops | bytes accessed | tf_op | source)
XLA Modules:
  0.0 901.3 jit_solution(6227883764159680559)
XLA Ops:
  9.1 5.1 collective-permute-start
  16.5 4.5 collective-permute-done
  27.1 9.3 %collective-permute-done.1 = f32[2,128,640]{2,1,0:T(8,128)} collective-permute-done((f32[2,128,640]{2,1,0:T(8,128)}, f32[2,128,640]{2,1,0:T(8,128)}, u32[]{:S(2)}, u32[]{:S(2)}) %collective-permute-start.1) | collective-permute-done | bytes 655392 | tf_op jit(solution)/shard_map/ppermute | solution.py:12
  42.7 551.6 %while.26 = (s32[]{:T(128)}, f32[2,640,640]{2,1,0:T(8,128)}, f32[640,640]{1,0:T(8,128)}, f32[2,4,128,128]{3,2,1,0:T(8,128)}, f32[128,128]{1,0:T(8,128)}, /*index...) while((s32[]{:T(128)}, f32[2,640,640]{2,1,0:T(8,128)}, ...), condition=%wide.region_8.9_spmd.clone, body=%wide.region_1.8_spmd.clone.sunk | while | flops 2172534784 | bytes 56100336 | solution.py:123
  50.2 3.2 dynamic_update_slice.200
  59.0 3.2 dynamic_update_slice.201
  67.5 3.2 dynamic_update_slice.202
  76.2 3.2 dynamic_update_slice.203
  93.4 3.2 dynamic_update_slice.205
  120.4 5.6 fusion.86
  132.8 5.4 convolution_bitcast_fusion.2
  138.2 3.5 add_reduce_fusion.3
  142.8 3.7 dynamic_update_slice.192
  147.6 3.7 dynamic_update_slice.193
  152.3 3.7 dynamic_update_slice.194
  157.1 3.7 dynamic_update_slice.195
  161.8 3.7 dynamic_update_slice.196
  166.7 3.6 dynamic_update_slice.197
  171.4 3.7 dynamic_update_slice.198
  176.1 3.7 dynamic_update_slice.199
  188.3 3.2 dynamic_update_slice.200
  205.6 3.2 dynamic_update_slice.202
  222.7 3.2 dynamic_update_slice.204
  231.4 3.2 dynamic_update_slice.205
  239.8 3.2 dynamic_update_slice.206
  258.4 5.6 fusion.86
  270.7 5.4 convolution_bitcast_fusion.2
  276.2 3.5 add_reduce_fusion.3
  280.8 3.7 dynamic_update_slice.192
  285.5 3.7 dynamic_update_slice.193
  290.3 3.7 dynamic_update_slice.194
  295.0 3.6 dynamic_update_slice.195
  299.7 3.7 dynamic_update_slice.196
  304.5 3.7 dynamic_update_slice.197
  309.3 3.7 dynamic_update_slice.198
  314.1 3.6 dynamic_update_slice.199
  334.8 3.2 dynamic_update_slice.201
  343.3 3.2 dynamic_update_slice.202
  369.1 3.2 dynamic_update_slice.205
  377.5 3.2 dynamic_update_slice.206
  396.1 5.6 fusion.86
  408.4 5.4 convolution_bitcast_fusion.2
  413.8 3.5 add_reduce_fusion.3
  418.4 3.4 dynamic_update_slice.192
  422.9 3.7 dynamic_update_slice.193
  427.6 3.7 dynamic_update_slice.194
  432.4 3.7 dynamic_update_slice.195
  437.1 3.5 dynamic_update_slice.196
  441.8 3.7 dynamic_update_slice.197
  446.6 3.7 dynamic_update_slice.198
  451.4 3.7 dynamic_update_slice.199
  463.5 3.2 dynamic_update_slice.200
  533.7 5.6 fusion.86
  546.1 5.4 convolution_bitcast_fusion.2
  551.6 3.5 add_reduce_fusion.3
  556.2 3.7 dynamic_update_slice.192
  560.9 3.7 dynamic_update_slice.193
  565.7 3.7 dynamic_update_slice.194
  570.4 3.7 dynamic_update_slice.195
  575.2 3.7 dynamic_update_slice.196
  580.1 3.7 dynamic_update_slice.197
  584.8 3.7 dynamic_update_slice.198
  589.6 3.7 dynamic_update_slice.199
  603.5 273.6 %all-reduce.3.cloned.1.call-done = (f32[2,4,128,128]{3,2,1,0:T(8,128)}, f32[128,128]{1,0:T(8,128)}) async-done(((f32[2,4,128,128]{3,2,1,0:T(8,128)}, f32[128,128]{1,0:T(8,128)}), (f32[2,4,128,128]{3,2,1,0:T(8,128)}, f32[128,128]{1,0:T(8,128)})) %all-reduce.3.cloned.1.call-update) | async-done | bytes 589840 | tf_op jit(solution)/shard_map/psum | solution.py:135
  (220 shorter events, 250.3 us)
Async XLA Ops:
  7.2 870.0 %all-reduce.3.cloned.1.call-start = ((), (), s32[]{:S(2)}) async-start(), calls=%async_computation | async-start | bytes 1179648 | tf_op jit(solution)/shard_map/psum | solution.py:135
  9.1 12.0 %collective-permute-start = (f32[2,512,128]{2,1,0:T(8,128)}, f32[2,512,128]{2,1,0:T(8,128)S(1)}, u32[]{:S(2)}, u32[]{:S(2)}) collective-permute-start(f32[2,512,128]{2,1,0:T(8,128)} %slice.512), channel_id=1, source_target_pairs={{1,0},{2,1},{3,2},{4,3},{5,4},{6,5},{7,6},{8,7},{9,8},{10,9},{11,1... | collective-permute-start | bytes 1572872 | tf_op jit(solution)/shard_map/ppermute | solution.py:12
  22.0 14.4 %collective-permute-start.1 = (f32[2,128,640]{2,1,0:T(8,128)}, f32[2,128,640]{2,1,0:T(8,128)}, u32[]{:S(2)}, u32[]{:S(2)}) collective-permute-start(f32[2,128,640]{2,1,0:T(8,128)} %slice.580), channel_id=1, source_target_pairs={{16,0},{32,16},{48,32},{64,48},{80,64},{96,80},{112,96},{128,112},... | collective-permute-start | bytes 1966088 | tf_op jit(solution)/shard_map/ppermute | solution.py:12
  39.4 3.3 copy-start.5
  165.5 14.3 %copy-start.1 = (f32[2,4,128,128]{3,2,1,0:T(8,128)S(1)}, f32[2,4,128,128]{3,2,1,0:T(8,128)}, u32[]{:S(2)}) copy-start(f32[2,4,128,128]{3,2,1,0:T(8,128)} %get-tuple-element.761) | copy-start | bytes 1572868 | tf_op jit(solution)/shard_map/while
  180.0 0.8 copy-start.2
  303.4 14.3 %copy-start.1 = (f32[2,4,128,128]{3,2,1,0:T(8,128)S(1)}, f32[2,4,128,128]{3,2,1,0:T(8,128)}, u32[]{:S(2)}) copy-start(f32[2,4,128,128]{3,2,1,0:T(8,128)} %get-tuple-element.761) | copy-start | bytes 1572868 | tf_op jit(solution)/shard_map/while
  317.9 0.8 copy-start.2
  440.7 14.4 %copy-start.1 = (f32[2,4,128,128]{3,2,1,0:T(8,128)S(1)}, f32[2,4,128,128]{3,2,1,0:T(8,128)}, u32[]{:S(2)}) copy-start(f32[2,4,128,128]{3,2,1,0:T(8,128)} %get-tuple-element.761) | copy-start | bytes 1572868 | tf_op jit(solution)/shard_map/while
  455.2 0.8 copy-start.2
  579.0 14.3 %copy-start.1 = (f32[2,4,128,128]{3,2,1,0:T(8,128)S(1)}, f32[2,4,128,128]{3,2,1,0:T(8,128)}, u32[]{:S(2)}) copy-start(f32[2,4,128,128]{3,2,1,0:T(8,128)} %get-tuple-element.761) | copy-start | bytes 1572868 | tf_op jit(solution)/shard_map/while
  593.5 0.8 copy-start.2
  594.3 288.9 %copy-start = (f32[2,640,640]{2,1,0:T(8,128)S(1)}, f32[2,640,640]{2,1,0:T(8,128)}, u32[]{:S(2)}) copy-start(f32[2,640,640]{2,1,0:T(8,128)} %get-tuple-element.405) | copy-start | bytes 9830404
  596.4 286.7 %collective-permute-start.2 = (f32[2,128,640]{2,1,0:T(8,128)}, f32[2,128,640]{2,1,0:T(8,128)}, u32[]{:S(2)}, u32[]{:S(2)}) collective-permute-start(f32[2,128,640]{2,1,0:T(8,128)} %slice.515), channel_id=1, source_target_pairs={{0,16},{16,32},{32,48},{48,64},{64,80},{80,96},{96,112},{112,128},... | collective-permute-start | bytes 1966088 | tf_op jit(solution)/shard_map/ppermute | solution.py:12
  600.3 277.8 %collective-permute-start.4 = (f32[128,640]{1,0:T(8,128)}, f32[128,640]{1,0:T(8,128)}, u32[]{:S(2)}, u32[]{:S(2)}) collective-permute-start(f32[128,640]{1,0:T(8,128)} %slice.520), channel_id=1, source_target_pairs={{0,16},{16,32},{32,48},{48,64},{64,80},{80,96},{96,112},{112,128},... | collective-permute-start | bytes 983048 | tf_op jit(solution)/shard_map/ppermute | solution.py:12
  878.0 8.4 copy-start.4
  880.9 7.6 collective-permute-start.5
  884.4 8.0 collective-permute-start.3
  890.2 2.4 copy-start.3
Sparse Core Ops, SparseCore 0:
  594.4 282.6 all-reduce.2
where the time goes:
time: 918 us; the launch traced here: 901 us
  waiting for transfers between devices  289 us (31%)
  local copies, waits for them, and re-layouts  284 us (31%)
  other arithmetic  134 us (15%)
  loops' own time  120 us (13%)
  matrix products  44.2 us (5%)
  starting transfers between devices  15.4 us (2%)
  between operations  14.2 us (2%)
    psum x1, waiting for transfers between devices, local(): lax.psum((probe_total, illum_total), ('wide', 'col'))  274 us
    another operation x1, loops' own time, local(): lax.fori_loop(0, block_total, run_block, initial)  120 us
    dynamic_update_slice x32, local copies, waits for them, and re-layouts, run_block(): lax.dynamic_update_slice(grad_ext, window + patch_grad[slot], (0, row_at,...  118 us
    dynamic_update_slice x32, local copies, waits for them, and re-layouts, run_block(): lax.dynamic_update_slice(weight_ext, spot + valid[slot] * power, (row_at,...  102 us
    add x28, other arithmetic, run_block(): spot + valid[slot] * power  46.1 us
    add x32, other arithmetic, run_block(): window + patch_grad[slot]  34.3 us
    while x44, local copies, waits for them, and re-layouts  33.2 us
    dot_general x4, matrix products, patch_terms(): jnp.einsum('bmdjk,dkcl->bmcjl', half, fwd_right, preferred_element_type=j...  22.4 us
  transfers between devices with their start and end apart: 7, of which 4 were waited for; matrix products, arithmetic and copies ran while one was open for 2% of the time, Pallas kernels for 0%

commit v1 on v0

v1 whole, which is shorter than its diff:
```python
import functools
import math

import jax
import jax.numpy as jnp
import ml_dtypes
import numpy as np
from jax import lax
from jax.experimental import pallas as pl
from jax.experimental.pallas import tpu as pltpu
from jax.sharding import PartitionSpec as P

MESH = pl.DeviceIdType.MESH
F32 = jnp.float32
BF16 = jnp.bfloat16
PATCH = 128
TILE = 512
EXT = TILE + PATCH
MODES = 4
RING = 16
PLANES = 2 * MODES + 1
ROWS = PATCH // RING
PAIR = 2

VMEM_SPEC = pl.BlockSpec(memory_space=pltpu.VMEM)
SMEM_SPEC = pl.BlockSpec(memory_space=pltpu.SMEM)
ANY_SPEC = pl.BlockSpec(memory_space=pl.ANY)


def left_table():
    indices = np.arange(PATCH)
    angles = (indices[:, None] * indices[None, :] % PATCH) * (2.0 * math.pi / PATCH)
    cosine = np.cos(angles) / math.sqrt(PATCH)
    sine = -np.sin(angles) / math.sqrt(PATCH)
    whole = np.block([[cosine, -sine], [sine, cosine]])
    return whole.astype(np.float32).astype(ml_dtypes.bfloat16)


def halo_in_kernel(obj, right, lower, diag, sent, got):
    w = lax.axis_index("wide")
    c = lax.axis_index("col")
    above, below = lax.rem(w + 15, 16), lax.rem(w + 1, 16)
    before, after = lax.rem(c + 15, 16), lax.rem(c + 1, 16)
    barrier = pltpu.get_barrier_semaphore()
    for target in ((w, after), (below, c), (below, after)):
        pl.semaphore_signal(barrier, inc=1, device_id=target, device_id_type=MESH)
    pl.semaphore_wait(barrier, 3)
    copies = (
        (obj.at[:, pl.ds(0, PATCH), :], lower, (above, c), w > 0, w < 15),
        (obj.at[:, :, pl.ds(0, PATCH)], right, (w, before), c > 0, c < 15),
        (
            obj.at[:, pl.ds(0, PATCH), pl.ds(0, PATCH)],
            diag,
            (above, before),
            (w > 0) & (c > 0),
            (w < 15) & (c < 15),
        ),
    )
    made = []
    for k, (source, dest, target, sends, gets) in enumerate(copies):
        copy = pltpu.make_async_remote_copy(
            source, dest, sent.at[k], got.at[k], device_id=target, device_id_type=MESH
        )
        pl.when(sends)(copy.start)
        made.append((copy, sends, gets))
    for copy, sends, gets in made:
        pl.when(gets)(copy.wait_recv)
        pl.when(sends)(copy.wait_send)


def halo_in(obj):
    return pl.pallas_call(
        halo_in_kernel,
        out_shape=[
            jax.ShapeDtypeStruct((2, TILE, PATCH), F32),
            jax.ShapeDtypeStruct((2, PATCH, TILE), F32),
            jax.ShapeDtypeStruct((2, PATCH, PATCH), F32),
        ],
        in_specs=[ANY_SPEC],
        out_specs=[ANY_SPEC] * 3,
        scratch_shapes=[pltpu.SemaphoreType.DMA((3,)), pltpu.SemaphoreType.DMA((3,))],
        compiler_params=pltpu.CompilerParams(collective_id=1, has_side_effects=True),
        name="halo_in",
    )(obj)


def patches_kernel(
    pos_ref, cnt_ref, probe_ref, lt_ref, rt_ref, amp_ref, obj, right, lower, diag,
    gw_ref, pg_ref, ext, sems,
):
    copies = []

    def fetch(source, dest):
        copy = pltpu.make_async_copy(source, dest, sems.at[len(copies)])
        copy.start()
        copies.append(copy)

    for ct in range(4):
        lanes = pl.ds(PATCH * ct, PATCH)
        fetch(obj.at[:, :, lanes], ext.at[:, ct, pl.ds(0, TILE), :])
        fetch(lower.at[:, :, lanes], ext.at[:, ct, pl.ds(TILE, PATCH), :])
    fetch(right, ext.at[:, 4, pl.ds(0, TILE), :])
    fetch(diag, ext.at[:, 4, pl.ds(TILE, PATCH), :])
    gw_ref[...] = jnp.zeros(gw_ref.shape, F32)
    pg_ref[...] = jnp.zeros(pg_ref.shape, F32)
    for copy in copies:
        copy.wait()

    @pl.when(lax.axis_index("wide") == 15)
    def _():
        ext[:, :, TILE:, :] = jnp.zeros((2, 5, PATCH, PATCH), F32)

    @pl.when(lax.axis_index("col") == 15)
    def _():
        ext[:, 4, :, :] = jnp.zeros((2, EXT, PATCH), F32)

    lane = lax.broadcasted_iota(jnp.int32, (PATCH, PATCH), 1)
    count = cnt_ref[0, 0]
    lt = lt_ref[...]
    rt = rt_ref[...]
    power = jnp.sum(probe_ref[...] * probe_ref[...], axis=(0, 1))

    def scatter(plane, row, ct, shift, value):
        turned = pltpu.roll(value, shift, 1)
        first = lane >= shift
        zero = jnp.zeros_like(turned)
        rows = pl.ds(row, PATCH)
        gw_ref[plane, ct, rows, :] += jnp.where(first, turned, zero)
        gw_ref[plane, ct + 1, rows, :] += jnp.where(first, zero, turned)

    def both_sides(left, stacked, right_side):
        half = jnp.dot(left, stacked, preferred_element_type=F32).astype(BF16)
        lanes = [slice(PATCH * m, PATCH * (m + 1)) for m in range(MODES)]
        turned = jnp.concatenate(
            [jnp.concatenate([half[:PATCH, at], half[PATCH:, at]], 1) for at in lanes], 0
        )
        return jnp.dot(turned, right_side, preferred_element_type=F32)

    def stack(re, im):
        return jnp.concatenate([jnp.concatenate(re, 1), jnp.concatenate(im, 1)], 0)

    def parts(values, m):
        rows = slice(PATCH * m, PATCH * (m + 1))
        return values[rows, :PATCH], values[rows, PATCH:]

    def step(index, carry):
        slots = [index * PAIR + u for u in range(PAIR)]
        info, waves = [], []
        for s in slots:
            row, at = pos_ref[s, 0], pos_ref[s, 1]
            ct, shift = lax.shift_right_logical(at, 7), lax.bitwise_and(at, 127)
            back = lax.bitwise_and(PATCH - shift, 127)
            rows = pl.ds(row, PATCH)
            patch = []
            for p in range(2):
                joined = jnp.where(lane >= shift, ext[p, ct, rows, :], ext[p, ct + 1, rows, :])
                patch.append(pltpu.roll(joined, back, 1))
            live = (s < count).astype(F32)
            info.append((row, ct, shift, live, patch))
            re, im = [], []
            for m in range(MODES):
                pr, pi = probe_ref[0, m], probe_ref[1, m]
                re.append((pr * patch[0] - pi * patch[1]).astype(BF16))
                im.append((pr * patch[1] + pi * patch[0]).astype(BF16))
            waves.append(stack(re, im))
        fars = [both_sides(lt, wave, rt) for wave in waves]
        residuals = []
        for u, s in enumerate(slots):
            intensity = jnp.zeros((PATCH, PATCH), F32)
            for m in range(MODES):
                fr, fi = parts(fars[u], m)
                intensity = intensity + fr * fr + fi * fi
            measured = amp_ref[s].astype(F32)
            factor = (measured * lax.rsqrt(jnp.maximum(intensity, 1.0)) - 1.0) * info[u][3]
            re, im = [], []
            for m in range(MODES):
                fr, fi = parts(fars[u], m)
                re.append((fr * factor).astype(BF16))
                im.append((fi * factor).astype(BF16))
            residuals.append(stack(re, im))
        updates = [both_sides(rt, residual, lt) for residual in residuals]
        for m in range(MODES):
            sum_re, sum_im = pg_ref[m], pg_ref[MODES + m]
            for u in range(PAIR):
                patch = info[u][4]
                ur, ui = parts(updates[u], m)
                sum_re = sum_re + patch[0] * ur + patch[1] * ui
                sum_im = sum_im + patch[0] * ui - patch[1] * ur
            pg_ref[m] = sum_re
            pg_ref[MODES + m] = sum_im
        lit = pg_ref[2 * MODES]
        for u in range(PAIR):
            patch = info[u][4]
            lit = lit + info[u][3] * (patch[0] * patch[0] + patch[1] * patch[1])
        pg_ref[2 * MODES] = lit
        for u in range(PAIR):
            row, ct, shift, live, _ = info[u]
            grad_re = jnp.zeros((PATCH, PATCH), F32)
            grad_im = grad_re
            for m in range(MODES):
                pr, pi = probe_ref[0, m], probe_ref[1, m]
                ur, ui = parts(updates[u], m)
                grad_re = grad_re + pr * ur + pi * ui
                grad_im = grad_im + pr * ui - pi * ur
            scatter(0, row, ct, shift, grad_re)
            scatter(1, row, ct, shift, grad_im)
            scatter(2, row, ct, shift, power * live)
        return carry

    lax.fori_loop(0, (count + PAIR - 1) // PAIR, step, 0)


def patches(pos, count, probe, amp, obj, right, lower, diag):
    table = left_table()
    return pl.pallas_call(
        patches_kernel,
        out_shape=[
            jax.ShapeDtypeStruct((3, 5, EXT, PATCH), F32),
            jax.ShapeDtypeStruct((PLANES, PATCH, PATCH), F32),
        ],
        in_specs=[SMEM_SPEC] * 2 + [VMEM_SPEC] * 4 + [ANY_SPEC] * 4,
        out_specs=[VMEM_SPEC] * 2,
        scratch_shapes=[pltpu.VMEM((2, 5, EXT, PATCH), F32), pltpu.SemaphoreType.DMA((10,))],
        compiler_params=pltpu.CompilerParams(vmem_limit_bytes=56 * 2**20),
        name="patches",
    )(pos, count, probe, jnp.asarray(table), jnp.asarray(table.T), amp, obj, right, lower, diag)


def exchange_kernel(
    pg, gw, total, from_above, from_left, from_diag,
    buf1, red1, buf2, red2, own, s1, r1, s2, r2, s3, r3, s4, r4, sh, rh,
):
    w = lax.axis_index("wide")
    c = lax.axis_index("col")
    above, below = lax.rem(w + 15, 16), lax.rem(w + 1, 16)
    before, after = lax.rem(c + 15, 16), lax.rem(c + 1, 16)

    def remote(source, dest, sent, got, target):
        return pltpu.make_async_remote_copy(
            source, dest, sent, got, device_id=target, device_id_type=MESH
        )

    def chunk(index):
        return pl.ds(pl.multiple_of(index * ROWS, ROWS), ROWS)

    barrier = pltpu.get_barrier_semaphore()
    for d in range(1, RING):
        for target in ((w, lax.rem(c + d, 16)), (lax.rem(w + d, 16), c)):
            pl.semaphore_signal(barrier, inc=1, device_id=target, device_id_type=MESH)
    pl.semaphore_signal(barrier, inc=1, device_id=(above, before), device_id_type=MESH)
    pl.semaphore_wait(barrier, 31)

    first = []
    for d in range(1, RING):
        p = lax.rem(c + d, 16)
        copy = remote(pg.at[:, chunk(p), :], buf1.at[d], s1.at[d], r1.at[d], (w, p))
        copy.start()
        first.append(copy)
    halos = (
        (gw.at[:, pl.ds(0, 4), pl.ds(TILE, PATCH), :], from_above, (below, c), w < 15, w > 0),
        (gw.at[:, 4, pl.ds(0, TILE), :], from_left, (w, after), c < 15, c > 0),
        (
            gw.at[:, 4, pl.ds(TILE, PATCH), :],
            from_diag,
            (below, after),
            (w < 15) & (c < 15),
            (w > 0) & (c > 0),
        ),
    )
    strips = []
    for k, (source, dest, target, sends, gets) in enumerate(halos):
        copy = remote(source, dest, sh.at[k], rh.at[k], target)
        pl.when(sends)(copy.start)
        strips.append((copy, sends, gets))
    acc = pg[:, chunk(c), :]
    for d in range(1, RING):
        first[d - 1].wait_recv()
        acc = acc + buf1[d]
    red1[...] = acc

    def to_owner(j):
        return remote(red1.at[j], buf2.at[w], s2.at[j], r2.at[w], (jnp.int32(j), c))

    def at_owner(j):
        return remote(red1.at[0], buf2.at[j], s2.at[0], r2.at[j], (w, c))

    def from_owner(d):
        return remote(red2, own.at[w], s3.at[d], r3.at[w], (lax.rem(w + d, 16), c))

    def at_user(j):
        return remote(red2, own.at[j], s3.at[0], r3.at[j], (w, c))

    for j in range(PLANES):
        @pl.when(w != j)
        def _(j=j):
            to_owner(j).start()

    @pl.when(w < PLANES)
    def _():
        buf2[w] = red1[w]
        for j in range(RING):
            @pl.when(w != j)
            def _(j=j):
                at_owner(j).wait_recv()
        acc2 = buf2[0]
        for j in range(1, RING):
            acc2 = acc2 + buf2[j]
        red2[...] = acc2
        for d in range(1, RING):
            from_owner(d).start()
        own[w] = acc2

    for j in range(PLANES):
        @pl.when(w != j)
        def _(j=j):
            at_user(j).wait_recv()

    fourth = []
    for d in range(1, RING):
        copy = remote(own, total.at[:, chunk(c), :], s4.at[d], r4.at[d], (w, lax.rem(c + d, 16)))
        copy.start()
        fourth.append(copy)
    total[:, chunk(c), :] = own[...]
    for copy in first:
        copy.wait_send()
    for j in range(PLANES):
        @pl.when(w != j)
        def _(j=j):
            to_owner(j).wait_send()

    @pl.when(w < PLANES)
    def _():
        for d in range(1, RING):
            from_owner(d).wait_send()

    for d in range(1, RING):
        p = lax.rem(c + 16 - d, 16)
        remote(own, total.at[:, chunk(p), :], s4.at[d], r4.at[d], (w, p)).wait_recv()
    for copy in fourth:
        copy.wait_send()
    for copy, sends, gets in strips:
        pl.when(gets)(copy.wait_recv)
        pl.when(sends)(copy.wait_send)


def exchange(pg, gw):
    ring = pltpu.SemaphoreType.DMA((RING,))
    three = pltpu.SemaphoreType.DMA((3,))
    return pl.pallas_call(
        exchange_kernel,
        out_shape=[
            jax.ShapeDtypeStruct((PLANES, PATCH, PATCH), F32),
            jax.ShapeDtypeStruct((3, 4, PATCH, PATCH), F32),
            jax.ShapeDtypeStruct((3, TILE, PATCH), F32),
            jax.ShapeDtypeStruct((3, PATCH, PATCH), F32),
        ],
        in_specs=[VMEM_SPEC, ANY_SPEC],
        out_specs=[VMEM_SPEC] + [ANY_SPEC] * 3,
        scratch_shapes=[
            pltpu.VMEM((RING, PLANES, ROWS, PATCH), F32),
            pltpu.VMEM((PLANES, ROWS, PATCH), F32),
            pltpu.VMEM((RING, ROWS, PATCH), F32),
            pltpu.VMEM((ROWS, PATCH), F32),
            pltpu.VMEM((PLANES, ROWS, PATCH), F32),
        ]
        + [ring] * 8
        + [three] * 2,
        compiler_params=pltpu.CompilerParams(collective_id=2, has_side_effects=True),
        name="exchange",
    )(pg, gw)


def finish_kernel(obj, gw, total, from_above, from_left, from_diag, new, direction):
    block = pl.program_id(0)
    w = lax.axis_index("wide")
    c = lax.axis_index("col")
    got_above = (block == 0) & (w > 0)
    got_left = c > 0
    got_diag = got_above & got_left

    @pl.when(block == 0)
    def _():
        direction[...] = total[: 2 * MODES] / jnp.sqrt(total[2 * MODES :] + 1.0)

    for ct in range(4):
        lanes = slice(PATCH * ct, PATCH * (ct + 1))
        sums = gw[:, ct]
        sums = sums + jnp.where(got_above, from_above[:, ct], 0.0)
        if ct == 0:
            sums = sums + jnp.where(got_left, from_left[...], 0.0)
            sums = sums + jnp.where(got_diag, from_diag[...], 0.0)
        weight = sums[2] + 1.0
        for p in range(2):
            new[p, :, lanes] = obj[p, :, lanes] + sums[p] / weight


def finish(obj, gw, total, from_above, from_left, from_diag):
    return pl.pallas_call(
        finish_kernel,
        grid=(4,),
        out_shape=[
            jax.ShapeDtypeStruct((2, TILE, TILE), F32),
            jax.ShapeDtypeStruct((2 * MODES, PATCH, PATCH), F32),
        ],
        in_specs=[
            pl.BlockSpec((2, PATCH, TILE), lambda i: (0, i, 0)),
            pl.BlockSpec((3, 4, PATCH, PATCH), lambda i: (0, 0, i, 0)),
            pl.BlockSpec((PLANES, PATCH, PATCH), lambda i: (0, 0, 0)),
            pl.BlockSpec((3, 4, PATCH, PATCH), lambda i: (0, 0, 0, 0)),
            pl.BlockSpec((3, PATCH, PATCH), lambda i: (0, i, 0)),
            pl.BlockSpec((3, PATCH, PATCH), lambda i: (0, 0, 0)),
        ],
        out_specs=[
            pl.BlockSpec((2, PATCH, TILE), lambda i: (0, i, 0)),
            pl.BlockSpec((2 * MODES, PATCH, PATCH), lambda i: (0, 0, 0)),
        ],
        name="finish",
    )(obj, gw, total, from_above, from_left, from_diag)


def local(object_field, probe_modes, amplitude, positions, slot_counts):
    slots = positions.shape[2]
    right, lower, diag = halo_in(object_field)
    gw, pg = patches(
        positions.reshape(slots, 2),
        slot_counts,
        probe_modes,
        amplitude.reshape(slots, PATCH, PATCH),
        object_field,
        right,
        lower,
        diag,
    )
    total, from_above, from_left, from_diag = exchange(pg, gw)
    new_object, direction = finish(object_field, gw, total, from_above, from_left, from_diag)
    return new_object, direction.reshape(probe_modes.shape)


def solution(mesh):
    placed = (
        P(None, "wide", "col"),
        P(),
        P("wide", "col", None, None, None),
        P("wide", "col", None, None),
        P("wide", "col"),
    )
    return jax.shard_map(
        local, mesh=mesh, in_specs=placed, out_specs=(P(None, "wide", "col"), P()), check_vma=False
    )
```

time: 918 us -> 154 us (0.17); the launches traced: 901 us -> 154 us
  waiting for transfers between devices: 289 us -> 0 us
  local copies, waits for them, and re-layouts: 284 us -> 1.36 us
  Pallas kernels: 0 us -> 151 us
  other arithmetic: 134 us -> 0 us
  loops' own time: 120 us -> 0 us
  matrix products: 44.2 us -> 0 us
  starting transfers between devices: 15.4 us -> 0 us
  between operations: 14.2 us -> 1.3 us
    psum x1 -> x0, waiting for transfers between devices: 274 us -> none  [local(): lax.psum((probe_total, illum_total), ('wide', 'col'))]
    dynamic_update_slice x64 -> x0, local copies, waits for them, and re-layouts: 220 us -> none  [the longest x32 118 us: run_block(): lax.dynamic_update_slice(grad_ext, window + patch_grad[slot], (0, row_at,...]
    pallas_call x0 -> x4, Pallas kernels: none -> 151 us  [the longest x1 99.6 us: exchange(): pl.pallas_call(exchange_kernel, out_shape=[jax.ShapeDtypeStruct((PLANES,...]
    another operation x1 -> x0, loops' own time: 120 us -> none  [local(): lax.fori_loop(0, block_total, run_block, initial)]
    add x70 -> x0, other arithmetic: 91.9 us -> none  [the longest x28 46.1 us: run_block(): spot + valid[slot] * power]
    dot_general x8 -> x0, matrix products: 44.2 us -> none  [the longest x4 22.4 us: patch_terms(): jnp.einsum('bmdjk,dkcl->bmcjl', half, fwd_right, preferred_element_type=j...]
    while x44 -> x0, local copies, waits for them, and re-layouts: 33.2 us -> none
    reduce_sum x9 -> x0, other arithmetic: 20.4 us -> none  [the longest x4 14 us: patch_terms(): term_re = jnp.sum(patch_re * update_re + patch_im * update_im, axis=0)]
  transfers between devices with their start and end apart: 7 -> 0, of which waited for: 4 -> 0; matrix products, arithmetic and copies ran while one was open for 2% -> 0% of each run, Pallas kernels for 0% -> 0%
where the time goes in v1:
time: 154 us
  Pallas kernels  151 us (98%)
    pallas_call x1, Pallas kernels, exchange(): pl.pallas_call(exchange_kernel, out_shape=[jax.ShapeDtypeStruct((PLANES,...  99.6 us
    pallas_call x1, Pallas kernels, patches(): pl.pallas_call(patches_kernel, out_shape=[jax.ShapeDtypeStruct((3, 5, EXT...  26.6 us
    pallas_call x1, Pallas kernels, halo_in(): pl.pallas_call(halo_in_kernel, out_shape=[jax.ShapeDtypeStruct((2, TILE,...  19.5 us
    pallas_call x1, Pallas kernels, finish(): pl.pallas_call(finish_kernel, grid=(4,), out_shape=[jax.ShapeDtypeStruct(...  5.39 us

profile of v1, /device:TPU:1, one launch (start us, length us, event | category | flops | bytes accessed | tf_op | source)
XLA Modules:
  0.0 153.7 jit_solution(11060173038546610301)
XLA Ops:
  1.3 1.4 copy.9.pos_ref
  2.6 19.5 %halo_in.1 = (f32[2,512,128]{2,1,0:T(8,128)}, f32[2,128,512]{2,1,0:T(8,128)}, f32[2,128,128]{2,1,0:T(8,128)}) custom-call(f32[2,512,512]{2,1,0:T(8,128)} %obj.5), custom_call_target="tpu_custom_call" | custom-call | tf_op jit(solution)/shard_map/halo_in/pallas_call | solution.py:72
  22.1 26.6 %patches.1 = (f32[3,5,640,128]{3,2,1,0:T(8,128)}, f32[9,128,128]{2,1,0:T(8,128)}) custom-call(s32[32,2]{1,0:T(8,128)} %copy.9.pos_ref, s32[1,1]{1,0:T(1,128)S(6)} %copy.10.cnt_ref, f32[2,4,128,128]{3,2,1,0:T(8,128)} %probe_ref.1, bf16[256,256]{1,0:T(8,128)(2,1)} %constant.4.clone.lt_ref, bf16[256,256]{1,0:T(8,128)(2,1)} %constant.5.clone.rt_ref, ...), custom_call_target="tpu_custom_call" | custom-call | tf_op jit(solution)/shard_map/patches/pallas_call | solution.py:215
  48.7 99.6 %exchange.1 = (f32[9,128,128]{2,1,0:T(8,128)}, f32[3,4,128,128]{3,2,1,0:T(8,128)}, f32[3,512,128]{2,1,0:T(8,128)}, f32[3,128,128]{2,1,0:T(8,128)}) custom-call(f32[9,128,128]{2,1,0:T(8,128)} %get-tuple-element.17.pg, f32[3,5,640,128]{3,2,1,0:T(8,128)} %get-tuple-element.16.gw), custom_call_target="tpu_custom_call" | custom-call | tf_op jit(solution)/shard_map/exchange/pallas_call | solution.py:349
  148.3 5.4 %finish.1 = (f32[2,512,512]{2,1,0:T(8,128)}, f32[8,128,128]{2,1,0:T(8,128)}) custom-call(f32[2,512,512]{2,1,0:T(8,128)} %obj.5, f32[3,5,640,128]{3,2,1,0:T(8,128)} %get-tuple-element.16.gw, f32[9,128,128]{2,1,0:T(8,128)} %get-tuple-element.18.total, f32[3,4,128,128]{3,2,1,0:T(8,128)} %get-tuple-element.19.from_above, ...), custom_call_target="tpu_custom_call" | custom-call | tf_op jit(solution)/shard_map/finish/pallas_call | solution.py:398

commit v2 on v1

v2 whole, which is shorter than its diff:
```python
import functools
import math

import jax
import jax.numpy as jnp
import ml_dtypes
import numpy as np
from jax import lax
from jax.experimental import pallas as pl
from jax.experimental.pallas import tpu as pltpu
from jax.sharding import PartitionSpec as P

MESH = pl.DeviceIdType.MESH
F32 = jnp.float32
BF16 = jnp.bfloat16
PATCH = 128
TILE = 512
EXT = TILE + PATCH
MODES = 4
RING = 16
PLANES = 2 * MODES + 1
ROWS = PATCH // RING
PAIR = 2
CHUNKS = 4

VMEM_SPEC = pl.BlockSpec(memory_space=pltpu.VMEM)
SMEM_SPEC = pl.BlockSpec(memory_space=pltpu.SMEM)
ANY_SPEC = pl.BlockSpec(memory_space=pl.ANY)


def left_table():
    indices = np.arange(PATCH)
    angles = (indices[:, None] * indices[None, :] % PATCH) * (2.0 * math.pi / PATCH)
    cosine = np.cos(angles) / math.sqrt(PATCH)
    sine = -np.sin(angles) / math.sqrt(PATCH)
    whole = np.block([[cosine, -sine], [sine, cosine]])
    return whole.astype(np.float32).astype(ml_dtypes.bfloat16)


def remote(source, dest, sent, got, target):
    return pltpu.make_async_remote_copy(
        source, dest, sent, got, device_id=target, device_id_type=MESH
    )


def greet(barrier, target):
    pl.semaphore_signal(barrier, inc=1, device_id=target, device_id_type=MESH)


def halo_in_kernel(
    obj, meta, right, lower, diag, meta_above, meta_left, meta_diag, passing,
    sent, got, sent_relay, got_relay,
):
    w = lax.axis_index("wide")
    c = lax.axis_index("col")
    y, k = lax.rem(w, 4), lax.div(w, 4)
    above, below = lax.rem(w + 15, 16), lax.rem(w + 1, 16)
    before, after = lax.rem(c + 15, 16), lax.rem(c + 1, 16)
    far_send, far_get = (y == 0) & (k > 0), (y == 3) & (k < 3)
    relays = (y == 3) & (k > 0)
    relay_from, relay_at = lax.rem(w + 13, 16), lax.rem(w + 3, 16)
    relay_to, got_from = lax.rem(w + 12, 16), lax.rem(w + 4, 16)
    barrier = pltpu.get_barrier_semaphore()
    for target in (
        (w, after), (below, c), (below, after), (w, before), (above, c), (above, before)
    ):
        greet(barrier, target)
    pl.when(relays)(lambda: greet(barrier, (relay_from, c)))
    pl.when(far_get)(lambda: greet(barrier, (got_from, c)))
    pl.semaphore_wait(barrier, 6 + jnp.where(far_send | relays, 1, 0))
    top = pl.ds(0, PATCH)
    size = PATCH // CHUNKS
    cuts = [pl.ds(j * size, size) for j in range(CHUNKS)]
    to_relay = [
        remote(
            obj.at[1, cut, :], passing.at[cut, :], sent_relay.at[j], got_relay.at[j], (relay_at, c)
        )
        for j, cut in enumerate(cuts)
    ]
    from_relay = [
        remote(
            passing.at[cut, :], lower.at[1, cut, :],
            sent_relay.at[CHUNKS + j], got_relay.at[CHUNKS + j], (relay_to, c),
        )
        for j, cut in enumerate(cuts)
    ]

    @pl.when(far_send)
    def _():
        for copy in to_relay:
            copy.start()

    ups, downs = w > 0, w < 15
    lefts, rights = c > 0, c < 15
    near_send = ups & jnp.logical_not(far_send)
    near_get = downs & jnp.logical_not(far_get)
    plain = (
        (obj.at[0, top, :], lower.at[0], (above, c), ups, downs),
        (obj.at[1, top, :], lower.at[1], (above, c), near_send, near_get),
        (obj.at[:, :, top], right, (w, before), lefts, rights),
        (obj.at[:, top, top], diag, (above, before), ups & lefts, downs & rights),
        (meta, meta_above, (below, c), downs, ups),
        (meta, meta_left, (w, after), rights, lefts),
        (meta, meta_diag, (below, after), downs & rights, ups & lefts),
    )
    made = []
    for j, (source, dest, target, sends, gets) in enumerate(plain):
        copy = remote(source, dest, sent.at[j], got.at[j], target)
        pl.when(sends)(copy.start)
        made.append((copy, sends, gets))

    @pl.when(relays)
    def _():
        for arrived, onward in zip(to_relay, from_relay):
            arrived.wait_recv()
            onward.start()

    for copy, sends, gets in made:
        pl.when(gets)(copy.wait_recv)
        pl.when(sends)(copy.wait_send)

    @pl.when(far_get)
    def _():
        for copy in from_relay:
            copy.wait_recv()

    @pl.when(relays)
    def _():
        for copy in from_relay:
            copy.wait_send()

    @pl.when(far_send)
    def _():
        for copy in to_relay:
            copy.wait_send()


def halo_in(obj, meta):
    note = jax.ShapeDtypeStruct(meta.shape, meta.dtype)
    return pl.pallas_call(
        halo_in_kernel,
        out_shape=[
            jax.ShapeDtypeStruct((2, TILE, PATCH), F32),
            jax.ShapeDtypeStruct((2, PATCH, TILE), F32),
            jax.ShapeDtypeStruct((2, PATCH, PATCH), F32),
            note,
            note,
            note,
            jax.ShapeDtypeStruct((PATCH, TILE), F32),
        ],
        in_specs=[ANY_SPEC] * 2,
        out_specs=[ANY_SPEC] * 7,
        scratch_shapes=[pltpu.SemaphoreType.DMA((7,))] * 2
        + [pltpu.SemaphoreType.DMA((2 * CHUNKS,))] * 2,
        compiler_params=pltpu.CompilerParams(collective_id=1, has_side_effects=True),
        name="halo_in",
    )(obj, meta)[:6]


def patches_kernel(
    meta_ref, above_ref, left_ref, diag_ref, probe_ref, lt_ref, rt_ref, amp_ref,
    obj, right, lower, diag, grad_ref, weight_ref, pg_ref, ext, spread, sems,
):
    copies = []

    def fetch(source, dest):
        copy = pltpu.make_async_copy(source, dest, sems.at[len(copies)])
        copy.start()
        copies.append(copy)

    for ct in range(4):
        lanes = pl.ds(PATCH * ct, PATCH)
        fetch(obj.at[:, :, lanes], ext.at[:, ct, pl.ds(0, TILE), :])
        fetch(lower.at[:, :, lanes], ext.at[:, ct, pl.ds(TILE, PATCH), :])
    fetch(right, ext.at[:, 4, pl.ds(0, TILE), :])
    fetch(diag, ext.at[:, 4, pl.ds(TILE, PATCH), :])
    grad_ref[...] = jnp.zeros(grad_ref.shape, F32)
    spread[...] = jnp.zeros(spread.shape, F32)
    pg_ref[...] = jnp.zeros(pg_ref.shape, F32)
    w = lax.axis_index("wide")
    c = lax.axis_index("col")
    lane = lax.broadcasted_iota(jnp.int32, (PATCH, PATCH), 1)
    count = meta_ref[2, 0]
    power = jnp.sum(probe_ref[...] * probe_ref[...], axis=(0, 1))

    def scatter(ref, row, at, value):
        ct, shift = lax.shift_right_logical(at, 7), lax.bitwise_and(at, 127)
        turned = pltpu.roll(value, shift, 1)
        first = lane >= shift
        zero = jnp.zeros_like(turned)
        rows = pl.ds(row, PATCH)
        ref[ct, rows, :] += jnp.where(first, turned, zero)
        ref[ct + 1, rows, :] += jnp.where(first, zero, turned)

    for ref, there, down, side in (
        (meta_ref, None, 0, 0),
        (above_ref, w > 0, TILE, 0),
        (left_ref, c > 0, 0, TILE),
        (diag_ref, (w > 0) & (c > 0), TILE, TILE),
    ):
        live_there = ref[2, 0] if there is None else jnp.where(there, ref[2, 0], 0)

        def weigh(s, carry, ref=ref, down=down, side=side):
            row, at = ref[0, s] + (PATCH - down), ref[1, s] + (PATCH - side)
            touches = None
            if down:
                touches = row > 0
            if side:
                touches = at > 0 if touches is None else touches & (at > 0)
            if touches is None:
                scatter(spread, row, at, power)
            else:
                pl.when(touches)(lambda: scatter(spread, row, at, power))
            return carry

        lax.fori_loop(0, live_there, weigh, 0)
    weight_ref[...] = spread[1:5, PATCH : PATCH + TILE, :]
    for copy in copies:
        copy.wait()

    @pl.when(w == 15)
    def _():
        ext[:, :, TILE:, :] = jnp.zeros((2, 5, PATCH, PATCH), F32)

    @pl.when(c == 15)
    def _():
        ext[:, 4, :, :] = jnp.zeros((2, EXT, PATCH), F32)

    lt = lt_ref[...]
    rt = rt_ref[...]

    def both_sides(left, stacked, right_side):
        half = jnp.dot(left, stacked, preferred_element_type=F32).astype(BF16)
        lanes = [slice(PATCH * m, PATCH * (m + 1)) for m in range(MODES)]
        turned = jnp.concatenate(
            [jnp.concatenate([half[:PATCH, at], half[PATCH:, at]], 1) for at in lanes], 0
        )
        return jnp.dot(turned, right_side, preferred_element_type=F32)

    def stack(re, im):
        return jnp.concatenate([jnp.concatenate(re, 1), jnp.concatenate(im, 1)], 0)

    def parts(values, m):
        rows = slice(PATCH * m, PATCH * (m + 1))
        return values[rows, :PATCH], values[rows, PATCH:]

    def step(index, carry):
        slots = [index * PAIR + u for u in range(PAIR)]
        info, waves = [], []
        for s in slots:
            row, at = meta_ref[0, s], meta_ref[1, s]
            ct, shift = lax.shift_right_logical(at, 7), lax.bitwise_and(at, 127)
            back = lax.bitwise_and(PATCH - shift, 127)
            rows = pl.ds(row, PATCH)
            patch = []
            for p in range(2):
                joined = jnp.where(lane >= shift, ext[p, ct, rows, :], ext[p, ct + 1, rows, :])
                patch.append(pltpu.roll(joined, back, 1))
            live = (s < count).astype(F32)
            info.append((row, at, None, live, patch))
            re, im = [], []
            for m in range(MODES):
                pr, pi = probe_ref[0, m], probe_ref[1, m]
                re.append((pr * patch[0] - pi * patch[1]).astype(BF16))
                im.append((pr * patch[1] + pi * patch[0]).astype(BF16))
            waves.append(stack(re, im))
        fars = [both_sides(lt, wave, rt) for wave in waves]
        residuals = []
        for u, s in enumerate(slots):
            intensity = jnp.zeros((PATCH, PATCH), F32)
            for m in range(MODES):
                fr, fi = parts(fars[u], m)
                intensity = intensity + fr * fr + fi * fi
            measured = amp_ref[s].astype(F32)
            factor = (measured * lax.rsqrt(jnp.maximum(intensity, 1.0)) - 1.0) * info[u][3]
            re, im = [], []
            for m in range(MODES):
                fr, fi = parts(fars[u], m)
                re.append((fr * factor).astype(BF16))
                im.append((fi * factor).astype(BF16))
            residuals.append(stack(re, im))
        updates = [both_sides(rt, residual, lt) for residual in residuals]
        for m in range(MODES):
            sum_re, sum_im = pg_ref[m], pg_ref[MODES + m]
            for u in range(PAIR):
                patch = info[u][4]
                ur, ui = parts(updates[u], m)
                sum_re = sum_re + patch[0] * ur + patch[1] * ui
                sum_im = sum_im + patch[0] * ui - patch[1] * ur
            pg_ref[m] = sum_re
            pg_ref[MODES + m] = sum_im
        lit = pg_ref[2 * MODES]
        for u in range(PAIR):
            patch = info[u][4]
            lit = lit + info[u][3] * (patch[0] * patch[0] + patch[1] * patch[1])
        pg_ref[2 * MODES] = lit
        for u in range(PAIR):
            row, at, _, live, _ = info[u]
            grad_re = jnp.zeros((PATCH, PATCH), F32)
            grad_im = grad_re
            for m in range(MODES):
                pr, pi = probe_ref[0, m], probe_ref[1, m]
                ur, ui = parts(updates[u], m)
                grad_re = grad_re + pr * ur + pi * ui
                grad_im = grad_im + pr * ui - pi * ur
            scatter(grad_ref.at[0], row, at, grad_re)
            scatter(grad_ref.at[1], row, at, grad_im)
        return carry

    lax.fori_loop(0, (count + PAIR - 1) // PAIR, step, 0)


def patches(metas, probe, amp, obj, right, lower, diag):
    table = left_table()
    return pl.pallas_call(
        patches_kernel,
        out_shape=[
            jax.ShapeDtypeStruct((2, 5, EXT, PATCH), F32),
            jax.ShapeDtypeStruct((4, TILE, PATCH), F32),
            jax.ShapeDtypeStruct((PLANES, PATCH, PATCH), F32),
        ],
        in_specs=[SMEM_SPEC] * 4 + [VMEM_SPEC] * 4 + [ANY_SPEC] * 4,
        out_specs=[VMEM_SPEC] * 3,
        scratch_shapes=[
            pltpu.VMEM((2, 5, EXT, PATCH), F32),
            pltpu.VMEM((6, EXT + PATCH, PATCH), F32),
            pltpu.SemaphoreType.DMA((10,)),
        ],
        compiler_params=pltpu.CompilerParams(vmem_limit_bytes=56 * 2**20),
        name="patches",
    )(*metas, probe, jnp.asarray(table), jnp.asarray(table.T), amp, obj, right, lower, diag)


def exchange_kernel(
    pg, grad, total, from_above, from_left, from_diag, passing,
    buf0, red0, buf1, red1, buf2, red2, buf3, own, res,
    s0, r0, s1, r1, s2, r2, s3, r3, s4, r4, s5, r5, s6, r6, sh, rh, sr, rr,
):
    w = lax.axis_index("wide")
    c = lax.axis_index("col")
    y, k = lax.rem(w, 4), lax.div(w, 4)
    core, chip = lax.rem(c, 2), lax.div(c, 2)
    sibling = (w, 2 * chip + 1 - core)
    above, below = lax.rem(w + 15, 16), lax.rem(w + 1, 16)
    before, after = lax.rem(c + 15, 16), lax.rem(c + 1, 16)
    far_send, far_get = (y == 3) & (k < 3), (y == 0) & (k > 0)
    relays = (y == 0) & (k < 3)
    relay_from, relay_at = lax.rem(w + 3, 16), lax.rem(w + 13, 16)
    relay_to, got_from = lax.rem(w + 4, 16), lax.rem(w + 12, 16)

    def rows(index, half):
        return pl.ds(pl.multiple_of(index * ROWS + half * (PATCH // 2), ROWS), ROWS)

    def planes(index):
        return pl.ds(index * 3, 3)

    chips = [(w, lax.rem(chip + d, 8) * 2 + core) for d in range(1, 8)]
    along_y = [(k * 4 + lax.rem(y + d, 4), c) for d in range(1, 4)]
    along_z = [(lax.rem(w + 4 * d, 16), c) for d in range(1, 4)]
    barrier = pltpu.get_barrier_semaphore()
    for target in [sibling] + chips + along_y + along_z:
        greet(barrier, target)
    for target in ((w, before), (above, c), (above, before)):
        greet(barrier, target)
    pl.when(relays)(lambda: greet(barrier, (relay_from, c)))
    pl.when(far_get)(lambda: greet(barrier, (got_from, c)))
    pl.semaphore_wait(barrier, 17 + jnp.where(far_send | relays, 1, 0))

    zeroth = []
    for d in range(1, 9):
        p = lax.rem(chip + d, 8)
        copy = remote(pg.at[:, rows(p, 1 - core), :], buf0.at[d - 1], s0.at[d - 1], r0.at[d - 1], sibling)
        copy.start()
        zeroth.append(copy)

    low = pl.ds(TILE, PATCH)
    size = PATCH // CHUNKS
    to_relay, from_relay = [], []
    for j in range(CHUNKS):
        cut = pl.ds(j * size, size)
        to_relay.append(remote(
            grad.at[1, pl.ds(0, 4), pl.ds(TILE + j * size, size), :], passing.at[:, cut, :],
            sr.at[j], rr.at[j], (relay_at, c),
        ))
        from_relay.append(remote(
            passing.at[:, cut, :], from_above.at[1, :, cut, :],
            sr.at[CHUNKS + j], rr.at[CHUNKS + j], (relay_to, c),
        ))
    ups, downs = w > 0, w < 15
    lefts, rights = c > 0, c < 15
    near_send = downs & jnp.logical_not(far_send)
    near_get = ups & jnp.logical_not(far_get)
    halos = (
        (grad.at[0, pl.ds(0, 4), low, :], from_above.at[0], (below, c), downs, ups),
        (grad.at[1, pl.ds(0, 4), low, :], from_above.at[1], (below, c), near_send, near_get),
        (grad.at[:, 4, pl.ds(0, TILE), :], from_left, (w, after), rights, lefts),
        (grad.at[:, 4, low, :], from_diag, (below, after), downs & rights, ups & lefts),
    )

    @pl.when(far_send)
    def _():
        for copy in to_relay:
            copy.start()

    strips = []
    for j, (source, dest, target, sends, gets) in enumerate(halos):
        copy = remote(source, dest, sh.at[j], rh.at[j], target)
        pl.when(sends)(copy.start)
        strips.append((copy, sends, gets))

    first = []
    for d in range(1, 8):
        p = lax.rem(chip + d, 8)
        zeroth[d - 1].wait_recv()
        red0[d - 1] = pg[:, rows(p, core), :] + buf0[d - 1]
        copy = remote(red0.at[d - 1], buf1.at[d], s1.at[d], r1.at[d], chips[d - 1])
        copy.start()
        first.append(copy)
    zeroth[7].wait_recv()
    acc = pg[:, rows(chip, core), :] + buf0[7]

    @pl.when(relays)
    def _():
        for arrived, onward in zip(to_relay, from_relay):
            arrived.wait_recv()
            onward.start()

    for d in range(1, 8):
        first[d - 1].wait_recv()
        acc = acc + buf1[d]
    red1[pl.ds(0, PLANES)] = acc
    red1[pl.ds(PLANES, 3)] = jnp.zeros((3, ROWS, PATCH), F32)
    second = []
    for d in range(1, 4):
        copy = remote(
            red1.at[planes(lax.rem(y + d, 4))], buf2.at[d], s2.at[d], r2.at[d], along_y[d - 1]
        )
        copy.start()
        second.append(copy)
    acc = red1[planes(y)]
    for d in range(1, 4):
        second[d - 1].wait_recv()
        acc = acc + buf2[d]
    buf3[k] = acc
    third = []
    for d in range(1, 4):
        copy = remote(buf3.at[k], buf3.at[k], s3.at[d], r3.at[d], along_z[d - 1])
        copy.start()
        third.append(copy)
    for d in range(1, 4):
        p = lax.rem(k + 4 - d, 4)
        remote(buf3.at[p], buf3.at[p], s3.at[d], r3.at[d], along_z[d - 1]).wait_recv()
    own[planes(y)] = buf3[0] + buf3[1] + buf3[2] + buf3[3]
    fourth = []
    for d in range(1, 4):
        copy = remote(own.at[planes(y)], own.at[planes(y)], s4.at[d], r4.at[d], along_y[d - 1])
        copy.start()
        fourth.append(copy)
    for d in range(1, 4):
        p = planes(lax.rem(y + 4 - d, 4))
        remote(own.at[p], own.at[p], s4.at[d], r4.at[d], along_y[d - 1]).wait_recv()
    lit = own[2 * MODES]
    res[...] = own[pl.ds(0, 2 * MODES)] / jnp.sqrt(lit + 1.0)[None]

    mine = rows(chip, core)
    fifth, sixth = [], []
    for d in range(1, 8):
        copy = remote(res, total.at[:, mine, :], s5.at[d], r5.at[d], chips[d - 1])
        copy.start()
        fifth.append(copy)
    copy = remote(res, total.at[:, mine, :], s6.at[0], r6.at[0], sibling)
    copy.start()
    sixth.append(copy)
    total[:, mine, :] = res[...]
    for d in range(1, 8):
        at = rows(lax.rem(chip + 8 - d, 8), core)
        remote(res, total.at[:, at, :], s5.at[d], r5.at[d], chips[d - 1]).wait_recv()
        copy = remote(total.at[:, at, :], total.at[:, at, :], s6.at[d], r6.at[d], sibling)
        copy.start()
        sixth.append(copy)
    for copy in zeroth + first + second + third + fourth + fifth:
        copy.wait_send()
    for d in range(8):
        at = rows(lax.rem(chip + 8 - d, 8), 1 - core)
        remote(res, total.at[:, at, :], s6.at[d], r6.at[d], sibling).wait_recv()
    for copy in sixth:
        copy.wait_send()
    for copy, sends, gets in strips:
        pl.when(gets)(copy.wait_recv)
        pl.when(sends)(copy.wait_send)

    @pl.when(far_get)
    def _():
        for copy in from_relay:
            copy.wait_recv()

    @pl.when(relays)
    def _():
        for copy in from_relay:
            copy.wait_send()

    @pl.when(far_send)
    def _():
        for copy in to_relay:
            copy.wait_send()


def exchange(pg, grad):
    eight = pltpu.SemaphoreType.DMA((8,))
    four = pltpu.SemaphoreType.DMA((4,))
    relayed = pltpu.SemaphoreType.DMA((2 * CHUNKS,))
    return pl.pallas_call(
        exchange_kernel,
        out_shape=[
            jax.ShapeDtypeStruct((2 * MODES, PATCH, PATCH), F32),
            jax.ShapeDtypeStruct((2, 4, PATCH, PATCH), F32),
            jax.ShapeDtypeStruct((2, TILE, PATCH), F32),
            jax.ShapeDtypeStruct((2, PATCH, PATCH), F32),
            jax.ShapeDtypeStruct((4, PATCH, PATCH), F32),
        ],
        in_specs=[VMEM_SPEC, ANY_SPEC],
        out_specs=[VMEM_SPEC] + [ANY_SPEC] * 4,
        scratch_shapes=[
            pltpu.VMEM((8, PLANES, ROWS, PATCH), F32),
            pltpu.VMEM((8, PLANES, ROWS, PATCH), F32),
            pltpu.VMEM((8, PLANES, ROWS, PATCH), F32),
            pltpu.VMEM((12, ROWS, PATCH), F32),
            pltpu.VMEM((4, 3, ROWS, PATCH), F32),
            pltpu.VMEM((3, ROWS, PATCH), F32),
            pltpu.VMEM((4, 3, ROWS, PATCH), F32),
            pltpu.VMEM((12, ROWS, PATCH), F32),
            pltpu.VMEM((2 * MODES, ROWS, PATCH), F32),
        ]
        + [eight] * 4
        + [four] * 6
        + [eight] * 4
        + [four] * 2
        + [relayed] * 2,
        compiler_params=pltpu.CompilerParams(collective_id=2, has_side_effects=True),
        name="exchange",
    )(pg, grad)[:4]


def finish_kernel(obj, grad, weight, total, from_above, from_left, from_diag, new, direction):
    block = pl.program_id(0)
    w = lax.axis_index("wide")
    c = lax.axis_index("col")
    got_above = (block == 0) & (w > 0)
    got_left = c > 0
    got_diag = got_above & got_left

    @pl.when(block == 0)
    def _():
        direction[...] = total[...]

    for ct in range(4):
        lanes = slice(PATCH * ct, PATCH * (ct + 1))
        sums = grad[:, ct]
        sums = sums + jnp.where(got_above, from_above[:, ct], 0.0)
        if ct == 0:
            sums = sums + jnp.where(got_left, from_left[...], 0.0)
            sums = sums + jnp.where(got_diag, from_diag[...], 0.0)
        scale = weight[ct] + 1.0
        for p in range(2):
            new[p, :, lanes] = obj[p, :, lanes] + sums[p] / scale


def finish(obj, grad, weight, total, from_above, from_left, from_diag):
    return pl.pallas_call(
        finish_kernel,
        grid=(4,),
        out_shape=[
            jax.ShapeDtypeStruct((2, TILE, TILE), F32),
            jax.ShapeDtypeStruct((2 * MODES, PATCH, PATCH), F32),
        ],
        in_specs=[
            pl.BlockSpec((2, PATCH, TILE), lambda i: (0, i, 0)),
            pl.BlockSpec((2, 4, PATCH, PATCH), lambda i: (0, 0, i, 0)),
            pl.BlockSpec((4, PATCH, PATCH), lambda i: (0, i, 0)),
            pl.BlockSpec((2 * MODES, PATCH, PATCH), lambda i: (0, 0, 0)),
            pl.BlockSpec((2, 4, PATCH, PATCH), lambda i: (0, 0, 0, 0)),
            pl.BlockSpec((2, PATCH, PATCH), lambda i: (0, i, 0)),
            pl.BlockSpec((2, PATCH, PATCH), lambda i: (0, 0, 0)),
        ],
        out_specs=[
            pl.BlockSpec((2, PATCH, TILE), lambda i: (0, i, 0)),
            pl.BlockSpec((2 * MODES, PATCH, PATCH), lambda i: (0, 0, 0)),
        ],
        name="finish",
    )(obj, grad, weight, total, from_above, from_left, from_diag)


def local(object_field, probe_modes, amplitude, positions, slot_counts):
    slots = positions.shape[2]
    meta = jnp.concatenate(
        [
            jnp.pad(positions.reshape(slots, 2).T, ((0, 0), (0, PATCH - slots))),
            jnp.broadcast_to(slot_counts, (6, PATCH)),
        ],
        0,
    )
    right, lower, diag, *others = halo_in(object_field, meta)
    grad, weight, pg = patches(
        (meta, *others),
        probe_modes,
        amplitude.reshape(slots, PATCH, PATCH),
        object_field,
        right,
        lower,
        diag,
    )
    total, from_above, from_left, from_diag = exchange(pg, grad)
    new_object, direction = finish(
        object_field, grad, weight, total, from_above, from_left, from_diag
    )
    return new_object, direction.reshape(probe_modes.shape)


def solution(mesh):
    placed = (
        P(None, "wide", "col"),
        P(),
        P("wide", "col", None, None, None),
        P("wide", "col", None, None),
        P("wide", "col"),
    )
    return jax.shard_map(
        local, mesh=mesh, in_specs=placed, out_specs=(P(None, "wide", "col"), P()), check_vma=False
    )
```

time: 154 us -> 119 us (0.77)
  Pallas kernels: 151 us -> 116 us
    pallas_call x2, Pallas kernels: 126 us -> 86.9 us  [the longest x1 78.6 us: exchange(): pl.pallas_call(exchange_kernel, out_shape=[jax.ShapeDtypeStruct((2 * MODE...]
    pallas_call x1, Pallas kernels: 19.5 us -> 23.9 us  [halo_in(): pl.pallas_call(halo_in_kernel, out_shape=[jax.ShapeDtypeStruct((2, TILE,...]
where the time goes in v2:
time: 119 us
  Pallas kernels  116 us (97%)
  between operations  1.3 us (1%)
  other arithmetic  1.28 us (1%)
    pallas_call x1, Pallas kernels, exchange(): pl.pallas_call(exchange_kernel, out_shape=[jax.ShapeDtypeStruct((2 * MODE...  78.6 us
    pallas_call x1, Pallas kernels, halo_in(): pl.pallas_call(halo_in_kernel, out_shape=[jax.ShapeDtypeStruct((2, TILE,...  23.9 us
    pallas_call x1, Pallas kernels, patches(): pl.pallas_call(patches_kernel, out_shape=[jax.ShapeDtypeStruct((2, 5, EXT...  8.28 us
    pallas_call x1, Pallas kernels, finish(): pl.pallas_call(finish_kernel, grid=(4,), out_shape=[jax.ShapeDtypeStruct(...  5.16 us

profile of v2, /device:TPU:1, one launch (start us, length us, event | category | flops | bytes accessed | tf_op | source)
XLA Modules:
  0.0 118.5 jit_solution(8944133596819312273)
XLA Ops:
  1.3 1.3 %pad_select_fusion.meta.meta_ref = s32[8,128]{1,0:T(8,128)} fusion(s32[2,32]{1,0:T(2,128)} %bitcast.8, s32[]{:T(128)} %bitcast.6), kind=kLoop, calls=%fused_computation.1 | loop fusion | flops 2048 | bytes 4356 | tf_op jit(solution)/shard_map/concatenate | solution.py:595
  2.6 23.9 %halo_in.1 = (f32[2,512,128]{2,1,0:T(8,128)}, f32[2,128,512]{2,1,0:T(8,128)}, f32[2,128,128]{2,1,0:T(8,128)}, s32[8,128]{1,0:T(8,128)}, s32[8,128]{1,0:T(8,128)}, /*index=5*/s32[8,128]{1,0:T(8,128)}, f32[128,512]{1,0:T(8,128)}) custom-call(f32[2,512,512]{2,1,0:T(8,128)} %obj.5, s32[8,128]{1,0:T(8,128)} %pad_select_fusion.meta.meta_ref), custom_call_target="tpu_custom_call" | custom-call | tf_op jit(solution)/shard_map/halo_in/pallas_call | solution.py:140
  26.5 8.3 %patches.1 = (f32[2,5,640,128]{3,2,1,0:T(8,128)}, f32[4,512,128]{2,1,0:T(8,128)}, f32[9,128,128]{2,1,0:T(8,128)}) custom-call(s32[8,128]{1,0:T(8,128)} %pad_select_fusion.meta.meta_ref, s32[8,128]{1,0:T(8,128)} %get-tuple-element.17.above_ref, s32[8,128]{1,0:T(8,128)} %get-tuple-element.18.left_ref, s32[8,128]{1,0:T(8,128)} %get-tuple-element.19.diag_ref, ...), custom_call_target="tpu_custom_call" | custom-call | tf_op jit(solution)/shard_map/patches/pallas_call | solution.py:315
  34.8 78.6 %exchange.1 = (f32[8,128,128]{2,1,0:T(8,128)}, f32[2,4,128,128]{3,2,1,0:T(8,128)}, f32[2,512,128]{2,1,0:T(8,128)}, f32[2,128,128]{2,1,0:T(8,128)}, f32[4,128,128]{2,1,0:T(8,128)}) custom-call(f32[9,128,128]{2,1,0:T(8,128)} %get-tuple-element.25.pg, f32[2,5,640,128]{3,2,1,0:T(8,128)} %get-tuple-element.23.grad), custom_call_target="tpu_custom_call" | custom-call | tf_op jit(solution)/shard_map/exchange/pallas_call | solution.py:512
  113.4 5.2 %finish.1 = (f32[2,512,512]{2,1,0:T(8,128)}, f32[8,128,128]{2,1,0:T(8,128)}) custom-call(f32[2,512,512]{2,1,0:T(8,128)} %obj.5, f32[2,5,640,128]{3,2,1,0:T(8,128)} %get-tuple-element.23.grad, f32[4,512,128]{2,1,0:T(8,128)} %get-tuple-element.24.weight, f32[8,128,128]{2,1,0:T(8,128)} %get-tuple-element.26.total, ...), custom_call_target="tpu_custom_call" | custom-call | tf_op jit(solution)/shard_map/finish/pallas_call | solution.py:569

commit v3 on v2

--- a/solution.py
+++ b/solution.py
@@ -22,6 +22,8 @@
 ROWS = PATCH // RING
 PAIR = 2
 CHUNKS = 4
+EARLY = 16
+INSIDE = TILE - PATCH
 
 VMEM_SPEC = pl.BlockSpec(memory_space=pltpu.VMEM)
 SMEM_SPEC = pl.BlockSpec(memory_space=pltpu.SMEM)
@@ -37,6 +39,117 @@
     return whole.astype(np.float32).astype(ml_dtypes.bfloat16)
 
 
+def plan_kernel(pos_ref, count_ref, meta_ref):
+    count = count_ref[0, 0]
+    low, high = jnp.int32(0), count - 1
+    for s in range(pos_ref.shape[1]):
+        row, at = pos_ref[0, s], pos_ref[1, s]
+        live = s < count
+        inner = live & (row <= INSIDE) & (at <= INSIDE)
+        place = jnp.where(inner, low, jnp.where(live, high, s))
+        meta_ref[0, place] = row
+        meta_ref[1, place] = at
+        meta_ref[3, place] = s
+        low = low + jnp.where(inner, 1, 0)
+        high = high - jnp.where(live & jnp.logical_not(inner), 1, 0)
+    for line in (0, 1, 3):
+        meta_ref[line, pos_ref.shape[1]] = 0
+    meta_ref[2, 0] = count
+    meta_ref[2, 1] = low
+
+
+def plan(positions, slot_counts):
+    return pl.pallas_call(
+        plan_kernel,
+        out_shape=jax.ShapeDtypeStruct((8, PATCH), jnp.int32),
+        in_specs=[SMEM_SPEC] * 2,
+        out_specs=SMEM_SPEC,
+        name="plan",
+    )(positions, slot_counts)
+
+
+def lanes_of():
+    return lax.broadcasted_iota(jnp.int32, (PATCH, PATCH), 1)
+
+
+def both_sides(left, stacked, right_side):
+    half = jnp.dot(left, stacked, preferred_element_type=F32).astype(BF16)
+    lanes = [slice(PATCH * m, PATCH * (m + 1)) for m in range(MODES)]
+    turned = jnp.concatenate(
+        [jnp.concatenate([half[:PATCH, at], half[PATCH:, at]], 1) for at in lanes], 0
+    )
+    return jnp.dot(turned, right_side, preferred_element_type=F32)
+
+
+def stack(re, im):
+    return jnp.concatenate([jnp.concatenate(re, 1), jnp.concatenate(im, 1)], 0)
+
+
+def parts(values, m):
+    rows = slice(PATCH * m, PATCH * (m + 1))
+    return values[rows, :PATCH], values[rows, PATCH:]
+
+
+def solve(slots, ext, last, probe_ref, lt, rt, amp_ref, pg_ref):
+    lane = lanes_of()
+    patches_of, waves = [], []
+    for s, row, at, live in slots:
+        ct, shift = lax.shift_right_logical(at, 7), lax.bitwise_and(at, 127)
+        back = lax.bitwise_and(PATCH - shift, 127)
+        beside = jnp.minimum(ct + 1, last)
+        rows = pl.ds(row, PATCH)
+        patch = []
+        for p in range(2):
+            joined = jnp.where(lane >= shift, ext[p, ct, rows, :], ext[p, beside, rows, :])
+            patch.append(pltpu.roll(joined, back, 1))
+        patches_of.append(patch)
+        re, im = [], []
+        for m in range(MODES):
+            pr, pi = probe_ref[0, m], probe_ref[1, m]
+            re.append((pr * patch[0] - pi * patch[1]).astype(BF16))
+            im.append((pr * patch[1] + pi * patch[0]).astype(BF16))
+        waves.append(stack(re, im))
+    fars = [both_sides(lt, wave, rt) for wave in waves]
+    residuals = []
+    for (s, row, at, live), far in zip(slots, fars):
+        intensity = jnp.zeros((PATCH, PATCH), F32)
+        for m in range(MODES):
+            fr, fi = parts(far, m)
+            intensity = intensity + fr * fr + fi * fi
+        measured = amp_ref[s].astype(F32)
+        factor = (measured * lax.rsqrt(jnp.maximum(intensity, 1.0)) - 1.0) * live
+        re, im = [], []
+        for m in range(MODES):
+            fr, fi = parts(far, m)
+            re.append((fr * factor).astype(BF16))
+            im.append((fi * factor).astype(BF16))
+        residuals.append(stack(re, im))
+    updates = [both_sides(rt, residual, lt) for residual in residuals]
+    for m in range(MODES):
+        sum_re, sum_im = pg_ref[m], pg_ref[MODES + m]
+        for patch, update in zip(patches_of, updates):
+            ur, ui = parts(update, m)
+            sum_re = sum_re + patch[0] * ur + patch[1] * ui
+            sum_im = sum_im + patch[0] * ui - patch[1] * ur
+        pg_ref[m] = sum_re
+        pg_ref[MODES + m] = sum_im
+    lit = pg_ref[2 * MODES]
+    for (s, row, at, live), patch in zip(slots, patches_of):
+        lit = lit + live * (patch[0] * patch[0] + patch[1] * patch[1])
+    pg_ref[2 * MODES] = lit
+    grads = []
+    for update in updates:
+        grad_re = jnp.zeros((PATCH, PATCH), F32)
+        grad_im = grad_re
+        for m in range(MODES):
+            pr, pi = probe_ref[0, m], probe_ref[1, m]
+            ur, ui = parts(update, m)
+            grad_re = grad_re + pr * ur + pi * ui
+            grad_im = grad_im + pr * ui - pi * ur
+        grads.append((grad_re, grad_im))
+    return grads
+
+
 def remote(source, dest, sent, got, target):
     return pltpu.make_async_remote_copy(
         source, dest, sent, got, device_id=target, device_id_type=MESH
@@ -48,9 +161,17 @@
 
 
 def halo_in_kernel(
-    obj, meta, right, lower, diag, meta_above, meta_left, meta_diag, passing,
-    sent, got, sent_relay, got_relay,
+    obj, meta, meta_ref, probe_ref, lt_ref, rt_ref, amp_ref,
+    right, lower, diag, meta_above, meta_left, meta_diag, passing, early_ref, pg_ref,
+    ext, fetched, sent, got, sent_relay, got_relay,
 ):
+    inward = []
+    for ct in range(4):
+        copy = pltpu.make_async_copy(
+            obj.at[:, :, pl.ds(PATCH * ct, PATCH)], ext.at[:, ct], fetched.at[ct]
+        )
+        copy.start()
+        inward.append(copy)
     w = lax.axis_index("wide")
     c = lax.axis_index("col")
     y, k = lax.rem(w, 4), lax.div(w, 4)
@@ -109,12 +230,35 @@
         pl.when(sends)(copy.start)
         made.append((copy, sends, gets))
 
+    pg_ref[...] = jnp.zeros(pg_ref.shape, F32)
+    lt = lt_ref[...]
+    rt = rt_ref[...]
+    inner = meta_ref[2, 1]
+    for copy in inward:
+        copy.wait()
+
+    def step(index, carry):
+        slots = []
+        for u in range(PAIR):
+            j = index * PAIR + u
+            row, at = jnp.minimum(meta_ref[0, j], INSIDE), jnp.minimum(meta_ref[1, j], INSIDE)
+            slots.append((meta_ref[3, j], row, at, (j < inner).astype(F32)))
+        grads = solve(slots, ext, 3, probe_ref, lt, rt, amp_ref, pg_ref)
+        for u, (grad_re, grad_im) in enumerate(grads):
+            early_ref[index * PAIR + u, 0] = grad_re
+            early_ref[index * PAIR + u, 1] = grad_im
+        return carry
+
+    steps = EARLY // PAIR
+    lax.fori_loop(0, steps // 2, step, 0)
+
     @pl.when(relays)
     def _():
         for arrived, onward in zip(to_relay, from_relay):
             arrived.wait_recv()
             onward.start()
 
+    lax.fori_loop(steps // 2, steps, step, 0)
     for copy, sends, gets in made:
         pl.when(gets)(copy.wait_recv)
         pl.when(sends)(copy.wait_send)
@@ -135,9 +279,9 @@
             copy.wait_send()
 
 
-def halo_in(obj, meta):
+def halo_in(obj, meta, probe, tables, amp):
     note = jax.ShapeDtypeStruct(meta.shape, meta.dtype)
-    return pl.pallas_call(
+    made = pl.pallas_call(
         halo_in_kernel,
         out_shape=[
             jax.ShapeDtypeStruct((2, TILE, PATCH), F32),
@@ -147,19 +291,26 @@
             note,
             note,
             jax.ShapeDtypeStruct((PATCH, TILE), F32),
+            jax.ShapeDtypeStruct((EARLY, 2, PATCH, PATCH), F32),
+            jax.ShapeDtypeStruct((PLANES, PATCH, PATCH), F32),
         ],
-        in_specs=[ANY_SPEC] * 2,
-        out_specs=[ANY_SPEC] * 7,
-        scratch_shapes=[pltpu.SemaphoreType.DMA((7,))] * 2
+        in_specs=[ANY_SPEC] * 2 + [SMEM_SPEC] + [VMEM_SPEC] * 4,
+        out_specs=[ANY_SPEC] * 7 + [VMEM_SPEC] * 2,
+        scratch_shapes=[pltpu.VMEM((2, 4, TILE, PATCH), F32), pltpu.SemaphoreType.DMA((4,))]
+        + [pltpu.SemaphoreType.DMA((7,))] * 2
         + [pltpu.SemaphoreType.DMA((2 * CHUNKS,))] * 2,
-        compiler_params=pltpu.CompilerParams(collective_id=1, has_side_effects=True),
+        compiler_params=pltpu.CompilerParams(
+            collective_id=1, has_side_effects=True, vmem_limit_bytes=56 * 2**20
+        ),
         name="halo_in",
-    )(obj, meta)[:6]
+    )(obj, meta, meta, probe, *tables, amp)
+    return made[:6], made[7], made[8]
 
 
 def patches_kernel(
     meta_ref, above_ref, left_ref, diag_ref, probe_ref, lt_ref, rt_ref, amp_ref,
-    obj, right, lower, diag, grad_ref, weight_ref, pg_ref, ext, spread, sems,
+    early_ref, early_pg, obj, right, lower, diag,
+    grad_ref, weight_ref, pg_ref, ext, spread, sems,
 ):
     copies = []
 
@@ -176,11 +327,12 @@
     fetch(diag, ext.at[:, 4, pl.ds(TILE, PATCH), :])
     grad_ref[...] = jnp.zeros(grad_ref.shape, F32)
     spread[...] = jnp.zeros(spread.shape, F32)
-    pg_ref[...] = jnp.zeros(pg_ref.shape, F32)
+    pg_ref[...] = early_pg[...]
     w = lax.axis_index("wide")
     c = lax.axis_index("col")
-    lane = lax.broadcasted_iota(jnp.int32, (PATCH, PATCH), 1)
+    lane = lanes_of()
     count = meta_ref[2, 0]
+    done = jnp.minimum(meta_ref[2, 1], EARLY)
     power = jnp.sum(probe_ref[...] * probe_ref[...], axis=(0, 1))
 
     def scatter(ref, row, at, value):
@@ -215,6 +367,13 @@
 
         lax.fori_loop(0, live_there, weigh, 0)
     weight_ref[...] = spread[1:5, PATCH : PATCH + TILE, :]
+
+    def place(j, carry):
+        for p in range(2):
+            scatter(grad_ref.at[p], meta_ref[0, j], meta_ref[1, j], early_ref[j, p])
+        return carry
+
+    lax.fori_loop(0, done, place, 0)
     for copy in copies:
         copy.wait()
 
@@ -229,89 +388,21 @@
     lt = lt_ref[...]
     rt = rt_ref[...]
 
-    def both_sides(left, stacked, right_side):
-        half = jnp.dot(left, stacked, preferred_element_type=F32).astype(BF16)
-        lanes = [slice(PATCH * m, PATCH * (m + 1)) for m in range(MODES)]
-        turned = jnp.concatenate(
-            [jnp.concatenate([half[:PATCH, at], half[PATCH:, at]], 1) for at in lanes], 0
-        )
-        return jnp.dot(turned, right_side, preferred_element_type=F32)
-
-    def stack(re, im):
-        return jnp.concatenate([jnp.concatenate(re, 1), jnp.concatenate(im, 1)], 0)
-
-    def parts(values, m):
-        rows = slice(PATCH * m, PATCH * (m + 1))
-        return values[rows, :PATCH], values[rows, PATCH:]
-
     def step(index, carry):
-        slots = [index * PAIR + u for u in range(PAIR)]
-        info, waves = [], []
-        for s in slots:
-            row, at = meta_ref[0, s], meta_ref[1, s]
-            ct, shift = lax.shift_right_logical(at, 7), lax.bitwise_and(at, 127)
-            back = lax.bitwise_and(PATCH - shift, 127)
-            rows = pl.ds(row, PATCH)
-            patch = []
-            for p in range(2):
-                joined = jnp.where(lane >= shift, ext[p, ct, rows, :], ext[p, ct + 1, rows, :])
-                patch.append(pltpu.roll(joined, back, 1))
-            live = (s < count).astype(F32)
-            info.append((row, at, None, live, patch))
-            re, im = [], []
-            for m in range(MODES):
-                pr, pi = probe_ref[0, m], probe_ref[1, m]
-                re.append((pr * patch[0] - pi * patch[1]).astype(BF16))
-                im.append((pr * patch[1] + pi * patch[0]).astype(BF16))
-            waves.append(stack(re, im))
-        fars = [both_sides(lt, wave, rt) for wave in waves]
-        residuals = []
-        for u, s in enumerate(slots):
-            intensity = jnp.zeros((PATCH, PATCH), F32)
-            for m in range(MODES):
-                fr, fi = parts(fars[u], m)
-                intensity = intensity + fr * fr + fi * fi
-            measured = amp_ref[s].astype(F32)
-            factor = (measured * lax.rsqrt(jnp.maximum(intensity, 1.0)) - 1.0) * info[u][3]
-            re, im = [], []
-            for m in range(MODES):
-                fr, fi = parts(fars[u], m)
-                re.append((fr * factor).astype(BF16))
-                im.append((fi * factor).astype(BF16))
-            residuals.append(stack(re, im))
-        updates = [both_sides(rt, residual, lt) for residual in residuals]
-        for m in range(MODES):
-            sum_re, sum_im = pg_ref[m], pg_ref[MODES + m]
-            for u in range(PAIR):
-                patch = info[u][4]
-                ur, ui = parts(updates[u], m)
-                sum_re = sum_re + patch[0] * ur + patch[1] * ui
-                sum_im = sum_im + patch[0] * ui - patch[1] * ur
-            pg_ref[m] = sum_re
-            pg_ref[MODES + m] = sum_im
-        lit = pg_ref[2 * MODES]
+        slots = []
         for u in range(PAIR):
-            patch = info[u][4]
-            lit = lit + info[u][3] * (patch[0] * patch[0] + patch[1] * patch[1])
-        pg_ref[2 * MODES] = lit
-        for u in range(PAIR):
-            row, at, _, live, _ = info[u]
-            grad_re = jnp.zeros((PATCH, PATCH), F32)
-            grad_im = grad_re
-            for m in range(MODES):
-                pr, pi = probe_ref[0, m], probe_ref[1, m]
-                ur, ui = parts(updates[u], m)
-                grad_re = grad_re + pr * ur + pi * ui
-                grad_im = grad_im + pr * ui - pi * ur
+            j = done + index * PAIR + u
+            slots.append((meta_ref[3, j], meta_ref[0, j], meta_ref[1, j], (j < count).astype(F32)))
+        grads = solve(slots, ext, 4, probe_ref, lt, rt, amp_ref, pg_ref)
+        for (s, row, at, live), (grad_re, grad_im) in zip(slots, grads):
             scatter(grad_ref.at[0], row, at, grad_re)
             scatter(grad_ref.at[1], row, at, grad_im)
         return carry
 
-    lax.fori_loop(0, (count + PAIR - 1) // PAIR, step, 0)
-
-
-def patches(metas, probe, amp, obj, right, lower, diag):
-    table = left_table()
+    lax.fori_loop(0, (count - done + PAIR - 1) // PAIR, step, 0)
+
+
+def patches(metas, probe, tables, amp, early, early_pg, obj, right, lower, diag):
     return pl.pallas_call(
         patches_kernel,
         out_shape=[
@@ -319,7 +410,7 @@
             jax.ShapeDtypeStruct((4, TILE, PATCH), F32),
             jax.ShapeDtypeStruct((PLANES, PATCH, PATCH), F32),
         ],
-        in_specs=[SMEM_SPEC] * 4 + [VMEM_SPEC] * 4 + [ANY_SPEC] * 4,
+        in_specs=[SMEM_SPEC] * 4 + [VMEM_SPEC] * 6 + [ANY_SPEC] * 4,
         out_specs=[VMEM_SPEC] * 3,
         scratch_shapes=[
             pltpu.VMEM((2, 5, EXT, PATCH), F32),
@@ -328,7 +419,7 @@
         ],
         compiler_params=pltpu.CompilerParams(vmem_limit_bytes=56 * 2**20),
         name="patches",
-    )(*metas, probe, jnp.asarray(table), jnp.asarray(table.T), amp, obj, right, lower, diag)
+    )(*metas, probe, *tables, amp, early, early_pg, obj, right, lower, diag)
 
 
 def exchange_kernel(
@@ -592,22 +683,16 @@
 
 def local(object_field, probe_modes, amplitude, positions, slot_counts):
     slots = positions.shape[2]
-    meta = jnp.concatenate(
-        [
-            jnp.pad(positions.reshape(slots, 2).T, ((0, 0), (0, PATCH - slots))),
-            jnp.broadcast_to(slot_counts, (6, PATCH)),
-        ],
-        0,
-    )
-    right, lower, diag, *others = halo_in(object_field, meta)
+    amp = amplitude.reshape(slots, PATCH, PATCH)
+    table = left_table()
+    tables = (jnp.asarray(table), jnp.asarray(table.T))
+    meta = plan(positions.reshape(slots, 2).T, slot_counts)
+    (right, lower, diag, *others), early, early_pg = halo_in(
+        object_field, meta, probe_modes, tables, amp
+    )
     grad, weight, pg = patches(
-        (meta, *others),
-        probe_modes,
-        amplitude.reshape(slots, PATCH, PATCH),
-        object_field,
-        right,
-        lower,
-        diag,
+        (meta, *others), probe_modes, tables, amp, early, early_pg,
+        object_field, right, lower, diag,
     )
     total, from_above, from_left, from_diag = exchange(pg, grad)
     new_object, direction = finish(

time: 119 us -> 115 us (0.966)
  Pallas kernels: 116 us -> 114 us
  other arithmetic: 1.28 us -> 0 us
    pallas_call x1, Pallas kernels: 78.6 us -> 68.1 us  [exchange(): pl.pallas_call(exchange_kernel, out_shape=[jax.ShapeDtypeStruct((2 * MODE...]
    pallas_call x1, Pallas kernels: 8.28 us -> 11.6 us  [patches(): pl.pallas_call(patches_kernel, out_shape=[jax.ShapeDtypeStruct((2, 5, EXT...]
    pallas_call x1, Pallas kernels: 23.9 us -> 27.2 us  [halo_in(): pl.pallas_call(halo_in_kernel, out_shape=[jax.ShapeDtypeStruct((2, TILE,...]
    pallas_call x0 -> x1, Pallas kernels: none -> 1.54 us  [plan(): pl.pallas_call(plan_kernel, out_shape=jax.ShapeDtypeStruct((8, PATCH), jn...]
    concatenate x1 -> x0, other arithmetic: 1.28 us -> none  [local(): jnp.concatenate([jnp.pad(positions.reshape(slots, 2).T, ((0, 0), (0, PATC...]
where the time goes in v3:
time: 115 us
  Pallas kernels  114 us (99%)
  between operations  1.31 us (1%)
    pallas_call x1, Pallas kernels, exchange(): pl.pallas_call(exchange_kernel, out_shape=[jax.ShapeDtypeStruct((2 * MODE...  68.1 us
    pallas_call x1, Pallas kernels, halo_in(): pl.pallas_call(halo_in_kernel, out_shape=[jax.ShapeDtypeStruct((2, TILE,...  27.2 us
    pallas_call x1, Pallas kernels, patches(): pl.pallas_call(patches_kernel, out_shape=[jax.ShapeDtypeStruct((2, 5, EXT...  11.6 us
    pallas_call x1, Pallas kernels, finish(): pl.pallas_call(finish_kernel, grid=(4,), out_shape=[jax.ShapeDtypeStruct(...  5.16 us

profile of v3, /device:TPU:1, one launch (start us, length us, event | category | flops | bytes accessed | tf_op | source)
XLA Modules:
  0.0 114.9 jit_solution(13767867519207119101)
XLA Ops:
  1.3 1.5 %plan.1.meta.meta_ref = s32[8,128]{1,0:T(8,128)} custom-call(s32[2,32]{1,0:T(2,128)} %bitcast.7, s32[1,1]{1,0:T(1,128)S(6)} %copy.9.count_ref), custom_call_target="tpu_custom_call" | custom-call | tf_op jit(solution)/shard_map/plan/pallas_call | solution.py:62
  2.8 27.2 %halo_in.1 = (f32[2,512,128]{2,1,0:T(8,128)}, f32[2,128,512]{2,1,0:T(8,128)}, f32[2,128,128]{2,1,0:T(8,128)}, s32[8,128]{1,0:T(8,128)}, s32[8,128]{1,0:T(8,128)}...) custom-call(f32[2,512,512]{2,1,0:T(8,128)} %obj.5, ...), custom_call_target="tpu_custom_call" | custom-call | tf_op jit(solution)/shard_map/halo_in/pallas_call | solution.py:284
  30.1 11.6 %patches.1 = (f32[2,5,640,128]{3,2,1,0:T(8,128)}, f32[4,512,128]{2,1,0:T(8,128)}, f32[9,128,128]{2,1,0:T(8,128)}) custom-call(s32[8,128]{1,0:T(8,128)} %plan.1.meta.meta_ref, s32[8,128]{1,0:T(8,128)} %get-tuple-element.19.above_ref, s32[8,128]{1,0:T(8,128)} %get-tuple-element.20.left_ref, s32[8,128]{1,0:T(8,128)} %get-tuple-element.21.diag_ref, ...), custom_call_target="tpu_custom_call" | custom-call | tf_op jit(solution)/shard_map/patches/pallas_call | solution.py:406
  41.7 68.1 %exchange.1 = (f32[8,128,128]{2,1,0:T(8,128)}, f32[2,4,128,128]{3,2,1,0:T(8,128)}, f32[2,512,128]{2,1,0:T(8,128)}, f32[2,128,128]{2,1,0:T(8,128)}, f32[4,128,128]{2,1,0:T(8,128)}) custom-call(f32[9,128,128]{2,1,0:T(8,128)} %get-tuple-element.29.pg, f32[2,5,640,128]{3,2,1,0:T(8,128)} %get-tuple-element.27.grad), custom_call_target="tpu_custom_call" | custom-call | tf_op jit(solution)/shard_map/exchange/pallas_call | solution.py:603
  109.8 5.2 %finish.1 = (f32[2,512,512]{2,1,0:T(8,128)}, f32[8,128,128]{2,1,0:T(8,128)}) custom-call(f32[2,512,512]{2,1,0:T(8,128)} %obj.5, f32[2,5,640,128]{3,2,1,0:T(8,128)} %get-tuple-element.27.grad, f32[4,512,128]{2,1,0:T(8,128)} %get-tuple-element.28.weight, f32[8,128,128]{2,1,0:T(8,128)} %get-tuple-element.30.total, ...), custom_call_target="tpu_custom_call" | custom-call | tf_op jit(solution)/shard_map/finish/pallas_call | solution.py:660

commit v4 on v3

--- a/solution.py
+++ b/solution.py
@@ -21,7 +21,8 @@
 PLANES = 2 * MODES + 1
 ROWS = PATCH // RING
 PAIR = 2
-CHUNKS = 4
+CHUNKS = 5
+DIRECT = PATCH - 2 * 8 * CHUNKS
 EARLY = 16
 INSIDE = TILE - PATCH
 
@@ -161,68 +162,77 @@
 
 
 def halo_in_kernel(
-    obj, meta, meta_ref, probe_ref, lt_ref, rt_ref, amp_ref,
-    right, lower, diag, meta_above, meta_left, meta_diag, passing, early_ref, pg_ref,
-    ext, fetched, sent, got, sent_relay, got_relay,
+    obj, meta, meta_ref, probe_ref, lt_ref, rt_ref, amp,
+    right, lower, diag, meta_above, meta_left, meta_diag, early, pg_ref,
+    ext, amp_ref, early_ref, passing, fetched, stored, sent, got, sent_to, got_to, sent_on, got_on,
 ):
-    inward = []
-    for ct in range(4):
-        copy = pltpu.make_async_copy(
-            obj.at[:, :, pl.ds(PATCH * ct, PATCH)], ext.at[:, ct], fetched.at[ct]
-        )
-        copy.start()
-        inward.append(copy)
     w = lax.axis_index("wide")
     c = lax.axis_index("col")
     y, k = lax.rem(w, 4), lax.div(w, 4)
     above, below = lax.rem(w + 15, 16), lax.rem(w + 1, 16)
     before, after = lax.rem(c + 15, 16), lax.rem(c + 1, 16)
     far_send, far_get = (y == 0) & (k > 0), (y == 3) & (k < 3)
-    relays = (y == 3) & (k > 0)
-    relay_from, relay_at = lax.rem(w + 13, 16), lax.rem(w + 3, 16)
-    relay_to, got_from = lax.rem(w + 12, 16), lax.rem(w + 4, 16)
+    relays = ((y == 3) | (y == 1)) & (k > 0)
+    route = jnp.where(y == 1, 1, 0)
+    onward_to = lax.rem(w + jnp.where(y == 1, 14, 12), 16)
     barrier = pltpu.get_barrier_semaphore()
     for target in (
         (w, after), (below, c), (below, after), (w, before), (above, c), (above, before)
     ):
         greet(barrier, target)
-    pl.when(relays)(lambda: greet(barrier, (relay_from, c)))
-    pl.when(far_get)(lambda: greet(barrier, (got_from, c)))
+    pl.when(relays & (y == 3))(lambda: greet(barrier, (lax.rem(w + 13, 16), c)))
+
+    @pl.when(far_get)
+    def _():
+        greet(barrier, (lax.rem(w + 4, 16), c))
+        greet(barrier, (lax.rem(w + 2, 16), c))
+
+    inward = [pltpu.make_async_copy(amp, amp_ref, fetched.at[4])]
+    for ct in range(4):
+        inward.append(pltpu.make_async_copy(
+            obj.at[:, :, pl.ds(PATCH * ct, PATCH)], ext.at[:, ct], fetched.at[ct]
+        ))
+    for copy in inward:
+        copy.start()
     pl.semaphore_wait(barrier, 6 + jnp.where(far_send | relays, 1, 0))
-    top = pl.ds(0, PATCH)
-    size = PATCH // CHUNKS
-    cuts = [pl.ds(j * size, size) for j in range(CHUNKS)]
-    to_relay = [
-        remote(
-            obj.at[1, cut, :], passing.at[cut, :], sent_relay.at[j], got_relay.at[j], (relay_at, c)
+
+    def strip(first, rows):
+        return pl.ds(first, rows)
+
+    def to_relay(r, j):
+        at = strip(DIRECT + 8 * (r * CHUNKS + j), 8)
+        return remote(
+            obj.at[:, at, :], passing.at[j], sent_to.at[r * CHUNKS + j], got_to.at[j],
+            (lax.rem(w + (1 if r else 3), 16), c),
         )
-        for j, cut in enumerate(cuts)
-    ]
-    from_relay = [
-        remote(
-            passing.at[cut, :], lower.at[1, cut, :],
-            sent_relay.at[CHUNKS + j], got_relay.at[CHUNKS + j], (relay_to, c),
+
+    def onward(r, j):
+        start = pl.multiple_of(DIRECT + 8 * (r * CHUNKS + j), 8)
+        return remote(
+            passing.at[j], lower.at[:, strip(start, 8), :],
+            sent_on.at[j], got_on.at[r * CHUNKS + j], (onward_to, c),
         )
-        for j, cut in enumerate(cuts)
-    ]
 
     @pl.when(far_send)
     def _():
-        for copy in to_relay:
-            copy.start()
+        for j in range(CHUNKS):
+            for r in range(2):
+                to_relay(r, j).start()
 
     ups, downs = w > 0, w < 15
     lefts, rights = c > 0, c < 15
     near_send = ups & jnp.logical_not(far_send)
     near_get = downs & jnp.logical_not(far_get)
+    top = pl.ds(0, PATCH)
+    some, rest = strip(0, DIRECT), strip(DIRECT, PATCH - DIRECT)
     plain = (
-        (obj.at[0, top, :], lower.at[0], (above, c), ups, downs),
-        (obj.at[1, top, :], lower.at[1], (above, c), near_send, near_get),
-        (obj.at[:, :, top], right, (w, before), lefts, rights),
-        (obj.at[:, top, top], diag, (above, before), ups & lefts, downs & rights),
         (meta, meta_above, (below, c), downs, ups),
         (meta, meta_left, (w, after), rights, lefts),
         (meta, meta_diag, (below, after), downs & rights, ups & lefts),
+        (obj.at[:, some, :], lower.at[:, some, :], (above, c), ups, downs),
+        (obj.at[:, rest, :], lower.at[:, rest, :], (above, c), near_send, near_get),
+        (obj.at[:, top, top], diag, (above, before), ups & lefts, downs & rights),
+        (obj.at[:, :, top], right, (w, before), lefts, rights),
     )
     made = []
     for j, (source, dest, target, sends, gets) in enumerate(plain):
@@ -236,6 +246,10 @@
     inner = meta_ref[2, 1]
     for copy in inward:
         copy.wait()
+
+    def put(index):
+        pair = pl.ds(index * PAIR, PAIR)
+        return pltpu.make_async_copy(early_ref.at[pair], early.at[pair], stored.at[index])
 
     def step(index, carry):
         slots = []
@@ -247,36 +261,38 @@
         for u, (grad_re, grad_im) in enumerate(grads):
             early_ref[index * PAIR + u, 0] = grad_re
             early_ref[index * PAIR + u, 1] = grad_im
+        put(index).start()
+
+        @pl.when(relays & (index > 0) & (index <= CHUNKS))
+        def _():
+            to_relay(0, index - 1).wait_recv()
+            onward(route, index - 1).start()
+
         return carry
 
-    steps = EARLY // PAIR
-    lax.fori_loop(0, steps // 2, step, 0)
-
-    @pl.when(relays)
-    def _():
-        for arrived, onward in zip(to_relay, from_relay):
-            arrived.wait_recv()
-            onward.start()
-
-    lax.fori_loop(steps // 2, steps, step, 0)
+    lax.fori_loop(0, EARLY // PAIR, step, 0)
+    for index in range(EARLY // PAIR):
+        put(index).wait()
     for copy, sends, gets in made:
         pl.when(gets)(copy.wait_recv)
         pl.when(sends)(copy.wait_send)
 
     @pl.when(far_get)
     def _():
-        for copy in from_relay:
-            copy.wait_recv()
+        for r in range(2):
+            for j in range(CHUNKS):
+                onward(r, j).wait_recv()
 
     @pl.when(relays)
     def _():
-        for copy in from_relay:
-            copy.wait_send()
+        for j in range(CHUNKS):
+            onward(0, j).wait_send()
 
     @pl.when(far_send)
     def _():
-        for copy in to_relay:
-            copy.wait_send()
+        for r in range(2):
+            for j in range(CHUNKS):
+                to_relay(r, j).wait_send()
 
 
 def halo_in(obj, meta, probe, tables, amp):
@@ -290,27 +306,34 @@
             note,
             note,
             note,
-            jax.ShapeDtypeStruct((PATCH, TILE), F32),
             jax.ShapeDtypeStruct((EARLY, 2, PATCH, PATCH), F32),
             jax.ShapeDtypeStruct((PLANES, PATCH, PATCH), F32),
         ],
-        in_specs=[ANY_SPEC] * 2 + [SMEM_SPEC] + [VMEM_SPEC] * 4,
-        out_specs=[ANY_SPEC] * 7 + [VMEM_SPEC] * 2,
-        scratch_shapes=[pltpu.VMEM((2, 4, TILE, PATCH), F32), pltpu.SemaphoreType.DMA((4,))]
+        in_specs=[ANY_SPEC] * 2 + [SMEM_SPEC] + [VMEM_SPEC] * 3 + [ANY_SPEC],
+        out_specs=[ANY_SPEC] * 7 + [VMEM_SPEC],
+        scratch_shapes=[
+            pltpu.VMEM((2, 4, TILE, PATCH), F32),
+            pltpu.VMEM(amp.shape, amp.dtype),
+            pltpu.VMEM((EARLY, 2, PATCH, PATCH), F32),
+            pltpu.VMEM((CHUNKS, 2, 8, TILE), F32),
+            pltpu.SemaphoreType.DMA((5,)),
+            pltpu.SemaphoreType.DMA((EARLY // PAIR,)),
+        ]
         + [pltpu.SemaphoreType.DMA((7,))] * 2
-        + [pltpu.SemaphoreType.DMA((2 * CHUNKS,))] * 2,
+        + [pltpu.SemaphoreType.DMA((2 * CHUNKS,)), pltpu.SemaphoreType.DMA((CHUNKS,))]
+        + [pltpu.SemaphoreType.DMA((CHUNKS,)), pltpu.SemaphoreType.DMA((2 * CHUNKS,))],
         compiler_params=pltpu.CompilerParams(
             collective_id=1, has_side_effects=True, vmem_limit_bytes=56 * 2**20
         ),
         name="halo_in",
     )(obj, meta, meta, probe, *tables, amp)
-    return made[:6], made[7], made[8]
+    return made[:6], made[6], made[7]
 
 
 def patches_kernel(
-    meta_ref, above_ref, left_ref, diag_ref, probe_ref, lt_ref, rt_ref, amp_ref,
-    early_ref, early_pg, obj, right, lower, diag,
-    grad_ref, weight_ref, pg_ref, ext, spread, sems,
+    meta_ref, above_ref, left_ref, diag_ref, probe_ref, lt_ref, rt_ref,
+    early_pg, amp, early, obj, right, lower, diag,
+    grad_ref, weight, pg_ref, ext, spread, amp_ref, early_ref, sems, stored,
 ):
     copies = []
 
@@ -319,6 +342,8 @@
         copy.start()
         copies.append(copy)
 
+    fetch(early, early_ref)
+    fetch(amp, amp_ref)
     for ct in range(4):
         lanes = pl.ds(PATCH * ct, PATCH)
         fetch(obj.at[:, :, lanes], ext.at[:, ct, pl.ds(0, TILE), :])
@@ -366,7 +391,11 @@
             return carry
 
         lax.fori_loop(0, live_there, weigh, 0)
-    weight_ref[...] = spread[1:5, PATCH : PATCH + TILE, :]
+    weights_out = pltpu.make_async_copy(
+        spread.at[pl.ds(1, 4), pl.ds(PATCH, TILE), :], weight, stored.at[0]
+    )
+    weights_out.start()
+    copies[0].wait()
 
     def place(j, carry):
         for p in range(2):
@@ -374,7 +403,7 @@
         return carry
 
     lax.fori_loop(0, done, place, 0)
-    for copy in copies:
+    for copy in copies[1:]:
         copy.wait()
 
     @pl.when(w == 15)
@@ -400,6 +429,7 @@
         return carry
 
     lax.fori_loop(0, (count - done + PAIR - 1) // PAIR, step, 0)
+    weights_out.wait()
 
 
 def patches(metas, probe, tables, amp, early, early_pg, obj, right, lower, diag):
@@ -410,22 +440,25 @@
             jax.ShapeDtypeStruct((4, TILE, PATCH), F32),
             jax.ShapeDtypeStruct((PLANES, PATCH, PATCH), F32),
         ],
-        in_specs=[SMEM_SPEC] * 4 + [VMEM_SPEC] * 6 + [ANY_SPEC] * 4,
-        out_specs=[VMEM_SPEC] * 3,
+        in_specs=[SMEM_SPEC] * 4 + [VMEM_SPEC] * 4 + [ANY_SPEC] * 6,
+        out_specs=[VMEM_SPEC, ANY_SPEC, VMEM_SPEC],
         scratch_shapes=[
             pltpu.VMEM((2, 5, EXT, PATCH), F32),
             pltpu.VMEM((6, EXT + PATCH, PATCH), F32),
-            pltpu.SemaphoreType.DMA((10,)),
+            pltpu.VMEM(amp.shape, amp.dtype),
+            pltpu.VMEM(early.shape, early.dtype),
+            pltpu.SemaphoreType.DMA((12,)),
+            pltpu.SemaphoreType.DMA((1,)),
         ],
         compiler_params=pltpu.CompilerParams(vmem_limit_bytes=56 * 2**20),
         name="patches",
-    )(*metas, probe, *tables, amp, early, early_pg, obj, right, lower, diag)
+    )(*metas, probe, *tables, early_pg, amp, early, obj, right, lower, diag)
 
 
 def exchange_kernel(
-    pg, grad, total, from_above, from_left, from_diag, passing,
-    buf0, red0, buf1, red1, buf2, red2, buf3, own, res,
-    s0, r0, s1, r1, s2, r2, s3, r3, s4, r4, s5, r5, s6, r6, sh, rh, sr, rr,
+    pg, grad, total, from_above, from_left, from_diag,
+    buf0, red0, buf1, red1, buf2, buf3, own, res, passing,
+    s0, r0, s1, r1, s2, r2, s3, r3, s4, r4, s5, r5, s6, r6, sh, rh, sent_to, got_to, sent_on, got_on,
 ):
     w = lax.axis_index("wide")
     c = lax.axis_index("col")
@@ -435,9 +468,9 @@
     above, below = lax.rem(w + 15, 16), lax.rem(w + 1, 16)
     before, after = lax.rem(c + 15, 16), lax.rem(c + 1, 16)
     far_send, far_get = (y == 3) & (k < 3), (y == 0) & (k > 0)
-    relays = (y == 0) & (k < 3)
-    relay_from, relay_at = lax.rem(w + 3, 16), lax.rem(w + 13, 16)
-    relay_to, got_from = lax.rem(w + 4, 16), lax.rem(w + 12, 16)
+    relays = ((y == 0) | (y == 2)) & (k < 3)
+    route = jnp.where(y == 2, 1, 0)
+    onward_to = lax.rem(w + jnp.where(y == 2, 2, 4), 16)
 
     def rows(index, half):
         return pl.ds(pl.multiple_of(index * ROWS + half * (PATCH // 2), ROWS), ROWS)
@@ -453,9 +486,13 @@
         greet(barrier, target)
     for target in ((w, before), (above, c), (above, before)):
         greet(barrier, target)
-    pl.when(relays)(lambda: greet(barrier, (relay_from, c)))
-    pl.when(far_get)(lambda: greet(barrier, (got_from, c)))
-    pl.semaphore_wait(barrier, 17 + jnp.where(far_send | relays, 1, 0))
+
+    @pl.when(far_get)
+    def _():
+        greet(barrier, (lax.rem(w + 12, 16), c))
+        greet(barrier, (lax.rem(w + 14, 16), c))
+
+    pl.semaphore_wait(barrier, 17 + jnp.where(relays, 1, 0))
 
     zeroth = []
     for d in range(1, 9):
@@ -464,41 +501,55 @@
         copy.start()
         zeroth.append(copy)
 
-    low = pl.ds(TILE, PATCH)
-    size = PATCH // CHUNKS
-    to_relay, from_relay = [], []
-    for j in range(CHUNKS):
-        cut = pl.ds(j * size, size)
-        to_relay.append(remote(
-            grad.at[1, pl.ds(0, 4), pl.ds(TILE + j * size, size), :], passing.at[:, cut, :],
-            sr.at[j], rr.at[j], (relay_at, c),
-        ))
-        from_relay.append(remote(
-            passing.at[:, cut, :], from_above.at[1, :, cut, :],
-            sr.at[CHUNKS + j], rr.at[CHUNKS + j], (relay_to, c),
-        ))
+    def to_relay(r, j):
+        at = TILE + DIRECT + 8 * (r * CHUNKS + j)
+        return remote(
+            grad.at[:, pl.ds(0, 4), pl.ds(at, 8), :], passing.at[j],
+            sent_to.at[r * CHUNKS + j], got_to.at[j], (lax.rem(w + (15 if r else 13), 16), c),
+        )
+
+    def onward(r, j):
+        at = pl.multiple_of(DIRECT + 8 * (r * CHUNKS + j), 8)
+        return remote(
+            passing.at[j], from_above.at[:, :, pl.ds(at, 8), :],
+            sent_on.at[j], got_on.at[r * CHUNKS + j], (onward_to, c),
+        )
+
+    def pass_on(chunks):
+        @pl.when(relays)
+        def _():
+            for j in chunks:
+                to_relay(0, j).wait_recv()
+                onward(route, j).start()
+
     ups, downs = w > 0, w < 15
     lefts, rights = c > 0, c < 15
     near_send = downs & jnp.logical_not(far_send)
     near_get = ups & jnp.logical_not(far_get)
-    halos = (
-        (grad.at[0, pl.ds(0, 4), low, :], from_above.at[0], (below, c), downs, ups),
-        (grad.at[1, pl.ds(0, 4), low, :], from_above.at[1], (below, c), near_send, near_get),
-        (grad.at[:, 4, pl.ds(0, TILE), :], from_left, (w, after), rights, lefts),
-        (grad.at[:, 4, low, :], from_diag, (below, after), downs & rights, ups & lefts),
-    )
-
-    @pl.when(far_send)
-    def _():
-        for copy in to_relay:
-            copy.start()
-
     strips = []
-    for j, (source, dest, target, sends, gets) in enumerate(halos):
-        copy = remote(source, dest, sh.at[j], rh.at[j], target)
+
+    def post(source, dest, target, sends, gets):
+        copy = remote(source, dest, sh.at[len(strips)], rh.at[len(strips)], target)
         pl.when(sends)(copy.start)
         strips.append((copy, sends, gets))
 
+    def post_rows(first, size, sends, gets):
+        post(
+            grad.at[:, pl.ds(0, 4), pl.ds(TILE + first, size), :],
+            from_above.at[:, :, pl.ds(first, size), :], (below, c), sends, gets,
+        )
+
+    def post_columns(first, size):
+        at = pl.ds(first, size)
+        post(grad.at[:, 4, at, :], from_left.at[:, at, :], (w, after), rights, lefts)
+
+    @pl.when(far_send)
+    def _():
+        for j in range(CHUNKS):
+            for r in range(2):
+                to_relay(r, j).start()
+
+    post_rows(DIRECT, 40, near_send, near_get)
     first = []
     for d in range(1, 8):
         p = lax.rem(chip + d, 8)
@@ -510,12 +561,12 @@
     zeroth[7].wait_recv()
     acc = pg[:, rows(chip, core), :] + buf0[7]
 
-    @pl.when(relays)
-    def _():
-        for arrived, onward in zip(to_relay, from_relay):
-            arrived.wait_recv()
-            onward.start()
-
+    post_rows(DIRECT + 40, 40, near_send, near_get)
+    post(
+        grad.at[:, 4, pl.ds(TILE, PATCH), :], from_diag, (below, after),
+        downs & rights, ups & lefts,
+    )
+    pass_on(range(2))
     for d in range(1, 8):
         first[d - 1].wait_recv()
         acc = acc + buf1[d]
@@ -528,6 +579,9 @@
         )
         copy.start()
         second.append(copy)
+    pass_on(range(2, CHUNKS))
+    post_rows(0, 24, downs, ups)
+    post_columns(0, 256)
     acc = red1[planes(y)]
     for d in range(1, 4):
         second[d - 1].wait_recv()
@@ -538,6 +592,8 @@
         copy = remote(buf3.at[k], buf3.at[k], s3.at[d], r3.at[d], along_z[d - 1])
         copy.start()
         third.append(copy)
+    post_rows(24, 24, downs, ups)
+    post_columns(256, 256)
     for d in range(1, 4):
         p = lax.rem(k + 4 - d, 4)
         remote(buf3.at[p], buf3.at[p], s3.at[d], r3.at[d], along_z[d - 1]).wait_recv()
@@ -582,24 +638,27 @@
 
     @pl.when(far_get)
     def _():
-        for copy in from_relay:
-            copy.wait_recv()
+        for r in range(2):
+            for j in range(CHUNKS):
+                onward(r, j).wait_recv()
 
     @pl.when(relays)
     def _():
-        for copy in from_relay:
-            copy.wait_send()
+        for j in range(CHUNKS):
+            onward(0, j).wait_send()
 
     @pl.when(far_send)
     def _():
-        for copy in to_relay:
-            copy.wait_send()
+        for r in range(2):
+            for j in range(CHUNKS):
+                to_relay(r, j).wait_send()
 
 
 def exchange(pg, grad):
     eight = pltpu.SemaphoreType.DMA((8,))
     four = pltpu.SemaphoreType.DMA((4,))
-    relayed = pltpu.SemaphoreType.DMA((2 * CHUNKS,))
+    ten = pltpu.SemaphoreType.DMA((2 * CHUNKS,))
+    five = pltpu.SemaphoreType.DMA((CHUNKS,))
     return pl.pallas_call(
         exchange_kernel,
         out_shape=[
@@ -607,29 +666,28 @@
             jax.ShapeDtypeStruct((2, 4, PATCH, PATCH), F32),
             jax.ShapeDtypeStruct((2, TILE, PATCH), F32),
             jax.ShapeDtypeStruct((2, PATCH, PATCH), F32),
-            jax.ShapeDtypeStruct((4, PATCH, PATCH), F32),
         ],
         in_specs=[VMEM_SPEC, ANY_SPEC],
-        out_specs=[VMEM_SPEC] + [ANY_SPEC] * 4,
+        out_specs=[VMEM_SPEC] + [ANY_SPEC] * 3,
         scratch_shapes=[
             pltpu.VMEM((8, PLANES, ROWS, PATCH), F32),
             pltpu.VMEM((8, PLANES, ROWS, PATCH), F32),
             pltpu.VMEM((8, PLANES, ROWS, PATCH), F32),
             pltpu.VMEM((12, ROWS, PATCH), F32),
             pltpu.VMEM((4, 3, ROWS, PATCH), F32),
-            pltpu.VMEM((3, ROWS, PATCH), F32),
             pltpu.VMEM((4, 3, ROWS, PATCH), F32),
             pltpu.VMEM((12, ROWS, PATCH), F32),
             pltpu.VMEM((2 * MODES, ROWS, PATCH), F32),
+            pltpu.VMEM((CHUNKS, 2, 4, 8, PATCH), F32),
         ]
         + [eight] * 4
         + [four] * 6
         + [eight] * 4
-        + [four] * 2
-        + [relayed] * 2,
+        + [eight] * 2
+        + [ten, five, five, ten],
         compiler_params=pltpu.CompilerParams(collective_id=2, has_side_effects=True),
         name="exchange",
-    )(pg, grad)[:4]
+    )(pg, grad)
 
 
 def finish_kernel(obj, grad, weight, total, from_above, from_left, from_diag, new, direction):

time: 115 us -> 96.1 us (0.84)
  Pallas kernels: 114 us -> 94.5 us
    pallas_call x1, Pallas kernels: 68.1 us -> 53.5 us  [exchange(): pl.pallas_call(exchange_kernel, out_shape=[jax.ShapeDtypeStruct((2 * MODE...]
    pallas_call x1, Pallas kernels: 11.6 us -> 7.83 us  [patches(): pl.pallas_call(patches_kernel, out_shape=[jax.ShapeDtypeStruct((2, 5, EXT...]
where the time goes in v4:
time: 96.1 us; the launch traced here: 95.8 us
  Pallas kernels  94.5 us (98%)
  between operations  1.31 us (1%)
    pallas_call x1, Pallas kernels, exchange(): pl.pallas_call(exchange_kernel, out_shape=[jax.ShapeDtypeStruct((2 * MODE...  53.5 us
    pallas_call x1, Pallas kernels, halo_in(): pl.pallas_call(halo_in_kernel, out_shape=[jax.ShapeDtypeStruct((2, TILE,...  26.5 us
    pallas_call x1, Pallas kernels, patches(): pl.pallas_call(patches_kernel, out_shape=[jax.ShapeDtypeStruct((2, 5, EXT...  7.83 us
    pallas_call x1, Pallas kernels, finish(): pl.pallas_call(finish_kernel, grid=(4,), out_shape=[jax.ShapeDtypeStruct(...  5.16 us

profile of v4, /device:TPU:1, one launch (start us, length us, event | category | flops | bytes accessed | tf_op | source)
XLA Modules:
  0.0 95.8 jit_solution(14633913759331598128)
XLA Ops:
  1.3 1.5 %plan.1.meta.meta_ref = s32[8,128]{1,0:T(8,128)} custom-call(s32[2,32]{1,0:T(2,128)} %bitcast.7, s32[1,1]{1,0:T(1,128)S(6)} %copy.9.count_ref), custom_call_target="tpu_custom_call" | custom-call | tf_op jit(solution)/shard_map/plan/pallas_call | solution.py:63
  2.8 26.5 %halo_in.1 = (f32[2,512,128]{2,1,0:T(8,128)}, f32[2,128,512]{2,1,0:T(8,128)}, f32[2,128,128]{2,1,0:T(8,128)}, s32[8,128]{1,0:T(8,128)}, s32[8,128]{1,0:T(8,128)}...) custom-call(f32[2,512,512]{2,1,0:T(8,128)} %obj.5, s32[8,128]{1,0:T(8,128)} %plan.1.meta.meta_ref, ...), custom_call_target="tpu_custom_call" | custom-call | tf_op jit(solution)/shard_map/halo_in/pallas_call | solution.py:300
  29.3 7.8 %patches.1 = (f32[2,5,640,128]{3,2,1,0:T(8,128)}, f32[4,512,128]{2,1,0:T(8,128)}, f32[9,128,128]{2,1,0:T(8,128)}) custom-call(s32[8,128]{1,0:T(8,128)} %plan.1.meta.meta_ref, s32[8,128]{1,0:T(8,128)} %get-tuple-element.19.above_ref, s32[8,128]{1,0:T(8,128)} %get-tuple-element.20.left_ref, s32[8,128]{1,0:T(8,128)} %get-tuple-element.21.diag_ref, ...), custom_call_target="tpu_custom_call" | custom-call | tf_op jit(solution)/shard_map/patches/pallas_call | solution.py:436
  37.2 53.5 %exchange.1 = (f32[8,128,128]{2,1,0:T(8,128)}, f32[2,4,128,128]{3,2,1,0:T(8,128)}, f32[2,512,128]{2,1,0:T(8,128)}, f32[2,128,128]{2,1,0:T(8,128)}) custom-call(f32[9,128,128]{2,1,0:T(8,128)} %get-tuple-element.29.pg, f32[2,5,640,128]{3,2,1,0:T(8,128)} %get-tuple-element.27.grad), custom_call_target="tpu_custom_call" | custom-call | tf_op jit(solution)/shard_map/exchange/pallas_call | solution.py:662
  90.7 5.2 %finish.1 = (f32[2,512,512]{2,1,0:T(8,128)}, f32[8,128,128]{2,1,0:T(8,128)}) custom-call(f32[2,512,512]{2,1,0:T(8,128)} %obj.5, f32[2,5,640,128]{3,2,1,0:T(8,128)} %get-tuple-element.27.grad, f32[4,512,128]{2,1,0:T(8,128)} %get-tuple-element.28.weight, f32[8,128,128]{2,1,0:T(8,128)} %get-tuple-element.30.total, ...), custom_call_target="tpu_custom_call" | custom-call | tf_op jit(solution)/shard_map/finish/pallas_call | solution.py:718

commit v5 on v4

--- a/solution.py
+++ b/solution.py
@@ -22,8 +22,12 @@
 ROWS = PATCH // RING
 PAIR = 2
 CHUNKS = 5
-DIRECT = PATCH - 2 * 8 * CHUNKS
-EARLY = 16
+ROUTES = 3
+DIRECT = PATCH - ROUTES * 8 * CHUNKS
+GROUP = 4
+FIRST = 16
+EARLY = 24
+REST = TILE - PATCH
 INSIDE = TILE - PATCH
 
 VMEM_SPEC = pl.BlockSpec(memory_space=pltpu.VMEM)
@@ -42,21 +46,32 @@
 
 def plan_kernel(pos_ref, count_ref, meta_ref):
     count = count_ref[0, 0]
-    low, high = jnp.int32(0), count - 1
+    slots = []
+    inner_count, upper_count = jnp.int32(0), jnp.int32(0)
     for s in range(pos_ref.shape[1]):
         row, at = pos_ref[0, s], pos_ref[1, s]
         live = s < count
-        inner = live & (row <= INSIDE) & (at <= INSIDE)
-        place = jnp.where(inner, low, jnp.where(live, high, s))
+        upper = live & (row <= INSIDE)
+        inner = upper & (at <= INSIDE)
+        slots.append((row, at, live, upper, inner))
+        inner_count = inner_count + jnp.where(inner, 1, 0)
+        upper_count = upper_count + jnp.where(upper, 1, 0)
+    low, middle, high = jnp.int32(0), inner_count, upper_count
+    for s, (row, at, live, upper, inner) in enumerate(slots):
+        outer = upper & jnp.logical_not(inner)
+        place = jnp.where(inner, low, jnp.where(outer, middle, jnp.where(live, high, s)))
         meta_ref[0, place] = row
         meta_ref[1, place] = at
         meta_ref[3, place] = s
         low = low + jnp.where(inner, 1, 0)
-        high = high - jnp.where(live & jnp.logical_not(inner), 1, 0)
+        middle = middle + jnp.where(outer, 1, 0)
+        high = high + jnp.where(live & jnp.logical_not(upper), 1, 0)
     for line in (0, 1, 3):
-        meta_ref[line, pos_ref.shape[1]] = 0
+        for past in range(pos_ref.shape[1], pos_ref.shape[1] + EARLY):
+            meta_ref[line, past] = 0
     meta_ref[2, 0] = count
-    meta_ref[2, 1] = low
+    meta_ref[2, 1] = inner_count
+    meta_ref[2, 2] = upper_count
 
 
 def plan(positions, slot_counts):
@@ -162,9 +177,10 @@
 
 
 def halo_in_kernel(
-    obj, meta, meta_ref, probe_ref, lt_ref, rt_ref, amp,
+    obj, meta, meta_ref, probe, left_side, right_side, amp,
     right, lower, diag, meta_above, meta_left, meta_diag, early, pg_ref,
-    ext, amp_ref, early_ref, passing, fetched, stored, sent, got, sent_to, got_to, sent_on, got_on,
+    ext, wide_ext, amp_ref, probe_ref, lt_ref, rt_ref, early_ref, passing, fetched, stored,
+    sent, got, sent_to, got_to, sent_on, got_on,
 ):
     w = lax.axis_index("wide")
     c = lax.axis_index("col")
@@ -172,29 +188,40 @@
     above, below = lax.rem(w + 15, 16), lax.rem(w + 1, 16)
     before, after = lax.rem(c + 15, 16), lax.rem(c + 1, 16)
     far_send, far_get = (y == 0) & (k > 0), (y == 3) & (k < 3)
-    relays = ((y == 3) | (y == 1)) & (k > 0)
-    route = jnp.where(y == 1, 1, 0)
-    onward_to = lax.rem(w + jnp.where(y == 1, 14, 12), 16)
+    relays = (y > 0) & (k > 0)
+    route = jnp.maximum(y - 1, 0)
+    onward_to = lax.rem(w + 15 - y, 16)
     barrier = pltpu.get_barrier_semaphore()
     for target in (
         (w, after), (below, c), (below, after), (w, before), (above, c), (above, before)
     ):
         greet(barrier, target)
-    pl.when(relays & (y == 3))(lambda: greet(barrier, (lax.rem(w + 13, 16), c)))
+    pl.when(relays & (y > 1))(lambda: greet(barrier, (lax.rem(w + 16 - y, 16), c)))
 
     @pl.when(far_get)
     def _():
-        greet(barrier, (lax.rem(w + 4, 16), c))
-        greet(barrier, (lax.rem(w + 2, 16), c))
-
-    inward = [pltpu.make_async_copy(amp, amp_ref, fetched.at[4])]
+        for r in range(ROUTES):
+            greet(barrier, (lax.rem(w + 2 + r, 16), c))
+
+    inward = [
+        pltpu.make_async_copy(source, dest, fetched.at[10 + j])
+        for j, (source, dest) in enumerate(
+            ((amp, amp_ref), (probe, probe_ref), (left_side, lt_ref), (right_side, rt_ref))
+        )
+    ]
     for ct in range(4):
         inward.append(pltpu.make_async_copy(
             obj.at[:, :, pl.ds(PATCH * ct, PATCH)], ext.at[:, ct], fetched.at[ct]
         ))
-    for copy in inward:
-        copy.start()
-    pl.semaphore_wait(barrier, 6 + jnp.where(far_send | relays, 1, 0))
+    beside = [
+        pltpu.make_async_copy(
+            obj.at[:, :, pl.ds(PATCH * ct, PATCH)], wide_ext.at[:, ct], fetched.at[5 + ct]
+        )
+        for ct in range(4)
+    ]
+    for copy in inward + beside:
+        copy.start()
+    pl.semaphore_wait(barrier, 6 + jnp.where(far_send, 2, jnp.where(relays, 1, 0)))
 
     def strip(first, rows):
         return pl.ds(first, rows)
@@ -203,7 +230,7 @@
         at = strip(DIRECT + 8 * (r * CHUNKS + j), 8)
         return remote(
             obj.at[:, at, :], passing.at[j], sent_to.at[r * CHUNKS + j], got_to.at[j],
-            (lax.rem(w + (1 if r else 3), 16), c),
+            (lax.rem(w + r + 1, 16), c),
         )
 
     def onward(r, j):
@@ -216,7 +243,7 @@
     @pl.when(far_send)
     def _():
         for j in range(CHUNKS):
-            for r in range(2):
+            for r in reversed(range(ROUTES)):
                 to_relay(r, j).start()
 
     ups, downs = w > 0, w < 15
@@ -232,7 +259,7 @@
         (obj.at[:, some, :], lower.at[:, some, :], (above, c), ups, downs),
         (obj.at[:, rest, :], lower.at[:, rest, :], (above, c), near_send, near_get),
         (obj.at[:, top, top], diag, (above, before), ups & lefts, downs & rights),
-        (obj.at[:, :, top], right, (w, before), lefts, rights),
+        (obj.at[:, :, top], wide_ext.at[:, 4], (w, before), lefts, rights),
     )
     made = []
     for j, (source, dest, target, sends, gets) in enumerate(plain):
@@ -241,45 +268,68 @@
         made.append((copy, sends, gets))
 
     pg_ref[...] = jnp.zeros(pg_ref.shape, F32)
-    lt = lt_ref[...]
-    rt = rt_ref[...]
     inner = meta_ref[2, 1]
     for copy in inward:
         copy.wait()
+    lt = lt_ref[...]
+    rt = rt_ref[...]
 
     def put(index):
-        pair = pl.ds(index * PAIR, PAIR)
+        pair = pl.ds(index * GROUP, GROUP)
         return pltpu.make_async_copy(early_ref.at[pair], early.at[pair], stored.at[index])
 
-    def step(index, carry):
+    def solve_some(index, first_slot, live_slots, tiles, last, columns):
         slots = []
-        for u in range(PAIR):
-            j = index * PAIR + u
-            row, at = jnp.minimum(meta_ref[0, j], INSIDE), jnp.minimum(meta_ref[1, j], INSIDE)
-            slots.append((meta_ref[3, j], row, at, (j < inner).astype(F32)))
-        grads = solve(slots, ext, 3, probe_ref, lt, rt, amp_ref, pg_ref)
+        for u in range(GROUP):
+            j = first_slot + u
+            row, at = jnp.minimum(meta_ref[0, j], INSIDE), jnp.minimum(meta_ref[1, j], columns)
+            slots.append((meta_ref[3, j], row, at, (j < live_slots).astype(F32)))
+        grads = solve(slots, tiles, last, probe_ref, lt, rt, amp_ref, pg_ref)
         for u, (grad_re, grad_im) in enumerate(grads):
-            early_ref[index * PAIR + u, 0] = grad_re
-            early_ref[index * PAIR + u, 1] = grad_im
+            early_ref[index * GROUP + u, 0] = grad_re
+            early_ref[index * GROUP + u, 1] = grad_im
         put(index).start()
 
-        @pl.when(relays & (index > 0) & (index <= CHUNKS))
-        def _():
-            to_relay(0, index - 1).wait_recv()
-            onward(route, index - 1).start()
-
+        for half in range(2):
+            @pl.when(relays & (index > 0) & (2 * index + half < CHUNKS + 2))
+            def _(j=2 * index + half - 2):
+                to_relay(0, j).wait_recv()
+                onward(route, j).start()
+
+    def first_step(index, carry):
+        solve_some(index, index * GROUP, inner, ext, 3, INSIDE)
         return carry
 
-    lax.fori_loop(0, EARLY // PAIR, step, 0)
-    for index in range(EARLY // PAIR):
+    lax.fori_loop(0, FIRST // GROUP, first_step, 0)
+    for copy in beside:
+        copy.wait()
+    pl.when(rights)(made[-1][0].wait_recv)
+
+    @pl.when(c == 15)
+    def _():
+        wide_ext[:, 4] = jnp.zeros((2, TILE, PATCH), F32)
+
+    keep = pltpu.make_async_copy(wide_ext.at[:, 4], right, fetched.at[9])
+    keep.start()
+    base = jnp.minimum(inner, FIRST)
+    upper = meta_ref[2, 2]
+
+    def next_step(index, carry):
+        solve_some(index, base + index * GROUP - FIRST, upper, wide_ext, 4, TILE - 1)
+        return carry
+
+    lax.fori_loop(FIRST // GROUP, EARLY // GROUP, next_step, 0)
+    keep.wait()
+    for index in range(EARLY // GROUP):
         put(index).wait()
-    for copy, sends, gets in made:
+    for copy, sends, gets in made[:-1]:
         pl.when(gets)(copy.wait_recv)
         pl.when(sends)(copy.wait_send)
+    pl.when(lefts)(made[-1][0].wait_send)
 
     @pl.when(far_get)
     def _():
-        for r in range(2):
+        for r in range(ROUTES):
             for j in range(CHUNKS):
                 onward(r, j).wait_recv()
 
@@ -290,7 +340,7 @@
 
     @pl.when(far_send)
     def _():
-        for r in range(2):
+        for r in range(ROUTES):
             for j in range(CHUNKS):
                 to_relay(r, j).wait_send()
 
@@ -309,19 +359,23 @@
             jax.ShapeDtypeStruct((EARLY, 2, PATCH, PATCH), F32),
             jax.ShapeDtypeStruct((PLANES, PATCH, PATCH), F32),
         ],
-        in_specs=[ANY_SPEC] * 2 + [SMEM_SPEC] + [VMEM_SPEC] * 3 + [ANY_SPEC],
+        in_specs=[ANY_SPEC] * 2 + [SMEM_SPEC] + [ANY_SPEC] * 4,
         out_specs=[ANY_SPEC] * 7 + [VMEM_SPEC],
         scratch_shapes=[
             pltpu.VMEM((2, 4, TILE, PATCH), F32),
+            pltpu.VMEM((2, 5, TILE, PATCH), F32),
             pltpu.VMEM(amp.shape, amp.dtype),
+            pltpu.VMEM(probe.shape, F32),
+            pltpu.VMEM(tables[0].shape, BF16),
+            pltpu.VMEM(tables[0].shape, BF16),
             pltpu.VMEM((EARLY, 2, PATCH, PATCH), F32),
             pltpu.VMEM((CHUNKS, 2, 8, TILE), F32),
-            pltpu.SemaphoreType.DMA((5,)),
-            pltpu.SemaphoreType.DMA((EARLY // PAIR,)),
+            pltpu.SemaphoreType.DMA((14,)),
+            pltpu.SemaphoreType.DMA((EARLY // GROUP,)),
         ]
         + [pltpu.SemaphoreType.DMA((7,))] * 2
-        + [pltpu.SemaphoreType.DMA((2 * CHUNKS,)), pltpu.SemaphoreType.DMA((CHUNKS,))]
-        + [pltpu.SemaphoreType.DMA((CHUNKS,)), pltpu.SemaphoreType.DMA((2 * CHUNKS,))],
+        + [pltpu.SemaphoreType.DMA((ROUTES * CHUNKS,)), pltpu.SemaphoreType.DMA((CHUNKS,))]
+        + [pltpu.SemaphoreType.DMA((CHUNKS,)), pltpu.SemaphoreType.DMA((ROUTES * CHUNKS,))],
         compiler_params=pltpu.CompilerParams(
             collective_id=1, has_side_effects=True, vmem_limit_bytes=56 * 2**20
         ),
@@ -331,9 +385,11 @@
 
 
 def patches_kernel(
-    meta_ref, above_ref, left_ref, diag_ref, probe_ref, lt_ref, rt_ref,
+    meta, meta_above, meta_left, meta_diag, probe, left_side, right_side,
     early_pg, amp, early, obj, right, lower, diag,
-    grad_ref, weight, pg_ref, ext, spread, amp_ref, early_ref, sems, stored,
+    pre, grad, weight, pg,
+    meta_ref, above_ref, left_ref, diag_ref, probe_ref, lt_ref, rt_ref, pg_ref, amp_ref, early_ref,
+    ext, grad_ref, spread, inner_ref, sems, stored,
 ):
     copies = []
 
@@ -342,7 +398,16 @@
         copy.start()
         copies.append(copy)
 
+    fetch(probe, probe_ref)
+    fetch(meta, meta_ref)
+    fetch(meta_above, above_ref)
+    fetch(meta_left, left_ref)
+    fetch(meta_diag, diag_ref)
+    at_first = len(copies)
     fetch(early, early_ref)
+    fetch(left_side, lt_ref)
+    fetch(right_side, rt_ref)
+    fetch(early_pg, pg_ref)
     fetch(amp, amp_ref)
     for ct in range(4):
         lanes = pl.ds(PATCH * ct, PATCH)
@@ -352,12 +417,14 @@
     fetch(diag, ext.at[:, 4, pl.ds(TILE, PATCH), :])
     grad_ref[...] = jnp.zeros(grad_ref.shape, F32)
     spread[...] = jnp.zeros(spread.shape, F32)
-    pg_ref[...] = early_pg[...]
+    for copy in copies[:at_first]:
+        copy.wait()
     w = lax.axis_index("wide")
     c = lax.axis_index("col")
     lane = lanes_of()
     count = meta_ref[2, 0]
-    done = jnp.minimum(meta_ref[2, 1], EARLY)
+    base = jnp.minimum(meta_ref[2, 1], FIRST)
+    done = jnp.minimum(meta_ref[2, 2], base + EARLY - FIRST)
     power = jnp.sum(probe_ref[...] * probe_ref[...], axis=(0, 1))
 
     def scatter(ref, row, at, value):
@@ -395,15 +462,16 @@
         spread.at[pl.ds(1, 4), pl.ds(PATCH, TILE), :], weight, stored.at[0]
     )
     weights_out.start()
-    copies[0].wait()
+    copies[at_first].wait()
 
     def place(j, carry):
+        held = jnp.where(j < base, j, j - base + FIRST)
         for p in range(2):
-            scatter(grad_ref.at[p], meta_ref[0, j], meta_ref[1, j], early_ref[j, p])
+            scatter(grad_ref.at[p], meta_ref[0, j], meta_ref[1, j], early_ref[held, p])
         return carry
 
     lax.fori_loop(0, done, place, 0)
-    for copy in copies[1:]:
+    for copy in copies[at_first + 1 :]:
         copy.wait()
 
     @pl.when(w == 15)
@@ -429,26 +497,57 @@
         return carry
 
     lax.fori_loop(0, (count - done + PAIR - 1) // PAIR, step, 0)
-    weights_out.wait()
+    outward = [weights_out]
+    low, top, between = pl.ds(TILE, PATCH), pl.ds(0, PATCH), pl.ds(PATCH, REST)
+    for source, dest in (
+        (pg_ref, pg),
+        (grad_ref.at[:, :, low, :], grad.at[:, :, low, :]),
+        (grad_ref.at[:, 4, pl.ds(0, TILE), :], grad.at[:, 4, pl.ds(0, TILE), :]),
+        (grad_ref.at[:, pl.ds(0, 4), top, :], grad.at[:, pl.ds(0, 4), top, :]),
+        (grad_ref.at[:, 0, between, :], grad.at[:, 0, between, :]),
+    ):
+        copy = pltpu.make_async_copy(source, dest, stored.at[len(outward)])
+        copy.start()
+        outward.append(copy)
+    inside = slice(PATCH, TILE)
+    for ct in range(1, 4):
+        scale = spread[ct + 1, PATCH + PATCH : PATCH + TILE, :] + 1.0
+        lanes = slice(PATCH * (ct - 1), PATCH * ct)
+        for p in range(2):
+            inner_ref[p, :, lanes] = ext[p, ct, inside, :] + grad_ref[p, ct, inside, :] / scale
+    copy = pltpu.make_async_copy(
+        inner_ref, pre.at[:, between, between], stored.at[len(outward)]
+    )
+    copy.start()
+    for copy in outward + [copy]:
+        copy.wait()
 
 
 def patches(metas, probe, tables, amp, early, early_pg, obj, right, lower, diag):
     return pl.pallas_call(
         patches_kernel,
         out_shape=[
+            jax.ShapeDtypeStruct((2, TILE, TILE), F32),
             jax.ShapeDtypeStruct((2, 5, EXT, PATCH), F32),
             jax.ShapeDtypeStruct((4, TILE, PATCH), F32),
             jax.ShapeDtypeStruct((PLANES, PATCH, PATCH), F32),
         ],
-        in_specs=[SMEM_SPEC] * 4 + [VMEM_SPEC] * 4 + [ANY_SPEC] * 6,
-        out_specs=[VMEM_SPEC, ANY_SPEC, VMEM_SPEC],
-        scratch_shapes=[
+        in_specs=[ANY_SPEC] * 14,
+        out_specs=[ANY_SPEC] * 4,
+        scratch_shapes=[pltpu.SMEM(metas[0].shape, jnp.int32)] * 4
+        + [
+            pltpu.VMEM(probe.shape, F32),
+            pltpu.VMEM(tables[0].shape, BF16),
+            pltpu.VMEM(tables[0].shape, BF16),
+            pltpu.VMEM((PLANES, PATCH, PATCH), F32),
+            pltpu.VMEM(amp.shape, amp.dtype),
+            pltpu.VMEM(early.shape, early.dtype),
+            pltpu.VMEM((2, 5, EXT, PATCH), F32),
             pltpu.VMEM((2, 5, EXT, PATCH), F32),
             pltpu.VMEM((6, EXT + PATCH, PATCH), F32),
-            pltpu.VMEM(amp.shape, amp.dtype),
-            pltpu.VMEM(early.shape, early.dtype),
-            pltpu.SemaphoreType.DMA((12,)),
-            pltpu.SemaphoreType.DMA((1,)),
+            pltpu.VMEM((2, REST, REST), F32),
+            pltpu.SemaphoreType.DMA((20,)),
+            pltpu.SemaphoreType.DMA((8,)),
         ],
         compiler_params=pltpu.CompilerParams(vmem_limit_bytes=56 * 2**20),
         name="patches",
@@ -456,8 +555,8 @@
 
 
 def exchange_kernel(
-    pg, grad, total, from_above, from_left, from_diag,
-    buf0, red0, buf1, red1, buf2, buf3, own, res, passing,
+    pg_far, grad, total, from_above, from_left, from_diag,
+    pg, loaded, buf0, red0, buf1, red1, buf2, buf3, own, res, passing,
     s0, r0, s1, r1, s2, r2, s3, r3, s4, r4, s5, r5, s6, r6, sh, rh, sent_to, got_to, sent_on, got_on,
 ):
     w = lax.axis_index("wide")
@@ -468,9 +567,9 @@
     above, below = lax.rem(w + 15, 16), lax.rem(w + 1, 16)
     before, after = lax.rem(c + 15, 16), lax.rem(c + 1, 16)
     far_send, far_get = (y == 3) & (k < 3), (y == 0) & (k > 0)
-    relays = ((y == 0) | (y == 2)) & (k < 3)
-    route = jnp.where(y == 2, 1, 0)
-    onward_to = lax.rem(w + jnp.where(y == 2, 2, 4), 16)
+    relays = (y < 3) & (k < 3)
+    route = jnp.maximum(2 - y, 0)
+    onward_to = lax.rem(w + 4 - y, 16)
 
     def rows(index, half):
         return pl.ds(pl.multiple_of(index * ROWS + half * (PATCH // 2), ROWS), ROWS)
@@ -489,9 +588,12 @@
 
     @pl.when(far_get)
     def _():
-        greet(barrier, (lax.rem(w + 12, 16), c))
-        greet(barrier, (lax.rem(w + 14, 16), c))
-
+        for r in range(ROUTES):
+            greet(barrier, (lax.rem(w + 12 + r, 16), c))
+
+    load = pltpu.make_async_copy(pg_far, pg, loaded)
+    load.start()
+    load.wait()
     pl.semaphore_wait(barrier, 17 + jnp.where(relays, 1, 0))
 
     zeroth = []
@@ -505,7 +607,7 @@
         at = TILE + DIRECT + 8 * (r * CHUNKS + j)
         return remote(
             grad.at[:, pl.ds(0, 4), pl.ds(at, 8), :], passing.at[j],
-            sent_to.at[r * CHUNKS + j], got_to.at[j], (lax.rem(w + (15 if r else 13), 16), c),
+            sent_to.at[r * CHUNKS + j], got_to.at[j], (lax.rem(w + 15 - r, 16), c),
         )
 
     def onward(r, j):
@@ -546,7 +648,7 @@
     @pl.when(far_send)
     def _():
         for j in range(CHUNKS):
-            for r in range(2):
+            for r in reversed(range(ROUTES)):
                 to_relay(r, j).start()
 
     post_rows(DIRECT, 40, near_send, near_get)
@@ -580,7 +682,8 @@
         copy.start()
         second.append(copy)
     pass_on(range(2, CHUNKS))
-    post_rows(0, 24, downs, ups)
+    post_rows(0, DIRECT, downs, ups)
+    post_rows(DIRECT + 80, 40, near_send, near_get)
     post_columns(0, 256)
     acc = red1[planes(y)]
     for d in range(1, 4):
@@ -592,7 +695,6 @@
         copy = remote(buf3.at[k], buf3.at[k], s3.at[d], r3.at[d], along_z[d - 1])
         copy.start()
         third.append(copy)
-    post_rows(24, 24, downs, ups)
     post_columns(256, 256)
     for d in range(1, 4):
         p = lax.rem(k + 4 - d, 4)
@@ -638,7 +740,7 @@
 
     @pl.when(far_get)
     def _():
-        for r in range(2):
+        for r in range(ROUTES):
             for j in range(CHUNKS):
                 onward(r, j).wait_recv()
 
@@ -649,7 +751,7 @@
 
     @pl.when(far_send)
     def _():
-        for r in range(2):
+        for r in range(ROUTES):
             for j in range(CHUNKS):
                 to_relay(r, j).wait_send()
 
@@ -657,8 +759,8 @@
 def exchange(pg, grad):
     eight = pltpu.SemaphoreType.DMA((8,))
     four = pltpu.SemaphoreType.DMA((4,))
-    ten = pltpu.SemaphoreType.DMA((2 * CHUNKS,))
-    five = pltpu.SemaphoreType.DMA((CHUNKS,))
+    many = pltpu.SemaphoreType.DMA((ROUTES * CHUNKS,))
+    few = pltpu.SemaphoreType.DMA((CHUNKS,))
     return pl.pallas_call(
         exchange_kernel,
         out_shape=[
@@ -667,9 +769,11 @@
             jax.ShapeDtypeStruct((2, TILE, PATCH), F32),
             jax.ShapeDtypeStruct((2, PATCH, PATCH), F32),
         ],
-        in_specs=[VMEM_SPEC, ANY_SPEC],
+        in_specs=[ANY_SPEC] * 2,
         out_specs=[VMEM_SPEC] + [ANY_SPEC] * 3,
         scratch_shapes=[
+            pltpu.VMEM((PLANES, PATCH, PATCH), F32),
+            pltpu.SemaphoreType.DMA,
             pltpu.VMEM((8, PLANES, ROWS, PATCH), F32),
             pltpu.VMEM((8, PLANES, ROWS, PATCH), F32),
             pltpu.VMEM((8, PLANES, ROWS, PATCH), F32),
@@ -684,59 +788,95 @@
         + [four] * 6
         + [eight] * 4
         + [eight] * 2
-        + [ten, five, five, ten],
-        compiler_params=pltpu.CompilerParams(collective_id=2, has_side_effects=True),
+        + [many, few, few, many],
+        compiler_params=pltpu.CompilerParams(
+            collective_id=2, has_side_effects=True, vmem_limit_bytes=56 * 2**20
+        ),
         name="exchange",
     )(pg, grad)
 
 
-def finish_kernel(obj, grad, weight, total, from_above, from_left, from_diag, new, direction):
-    block = pl.program_id(0)
-    w = lax.axis_index("wide")
-    c = lax.axis_index("col")
-    got_above = (block == 0) & (w > 0)
-    got_left = c > 0
-    got_diag = got_above & got_left
-
-    @pl.when(block == 0)
-    def _():
-        direction[...] = total[...]
-
+def finish_kernel(
+    pre, obj, grad, weight, total, from_above, from_left, from_diag, new, direction,
+    obj_top, obj_left, grad_top, grad_left, weight_top, weight_left, above, left, corner,
+    new_top, new_left, held, sems, stored,
+):
+    del pre
+    top, between, tiles = pl.ds(0, PATCH), pl.ds(PATCH, REST), pl.ds(0, 4)
+    copies = []
+    for source, dest in (
+        (obj.at[:, between, top], obj_left),
+        (grad.at[:, 0, between, :], grad_left),
+        (weight.at[0, between, :], weight_left),
+        (from_left, left),
+        (total, held),
+        (obj.at[:, top, :], obj_top),
+        (grad.at[:, tiles, top, :], grad_top),
+        (weight.at[:, top, :], weight_top),
+        (from_above, above),
+        (from_diag, corner),
+    ):
+        copy = pltpu.make_async_copy(source, dest, sems.at[len(copies)])
+        copy.start()
+        copies.append(copy)
+    got_above, got_left = lax.axis_index("wide") > 0, lax.axis_index("col") > 0
+    for copy in copies[:4]:
+        copy.wait()
+    scale = weight_left[...] + 1.0
+    for p in range(2):
+        sums = grad_left[p] + jnp.where(got_left, left[p, PATCH:], 0.0)
+        new_left[p] = obj_left[p] + sums / scale
+    left_out = pltpu.make_async_copy(new_left, new.at[:, between, top], stored.at[1])
+    left_out.start()
+    copies[4].wait()
+    whole = pltpu.make_async_copy(held, direction, stored.at[0])
+    whole.start()
+    for copy in copies[5:]:
+        copy.wait()
     for ct in range(4):
         lanes = slice(PATCH * ct, PATCH * (ct + 1))
-        sums = grad[:, ct]
-        sums = sums + jnp.where(got_above, from_above[:, ct], 0.0)
-        if ct == 0:
-            sums = sums + jnp.where(got_left, from_left[...], 0.0)
-            sums = sums + jnp.where(got_diag, from_diag[...], 0.0)
-        scale = weight[ct] + 1.0
+        scale = weight_top[ct] + 1.0
         for p in range(2):
-            new[p, :, lanes] = obj[p, :, lanes] + sums[p] / scale
-
-
-def finish(obj, grad, weight, total, from_above, from_left, from_diag):
+            sums = grad_top[p, ct] + jnp.where(got_above, above[p, ct], 0.0)
+            if ct == 0:
+                sums = sums + jnp.where(got_left, left[p, :PATCH], 0.0)
+                sums = sums + jnp.where(got_above & got_left, corner[p], 0.0)
+            new_top[p, :, lanes] = obj_top[p, :, lanes] + sums / scale
+    top_out = pltpu.make_async_copy(new_top, new.at[:, top, :], stored.at[2])
+    top_out.start()
+    for copy in (whole, left_out, top_out):
+        copy.wait()
+
+
+def finish(pre, obj, grad, weight, total, from_above, from_left, from_diag):
     return pl.pallas_call(
         finish_kernel,
-        grid=(4,),
         out_shape=[
             jax.ShapeDtypeStruct((2, TILE, TILE), F32),
             jax.ShapeDtypeStruct((2 * MODES, PATCH, PATCH), F32),
         ],
-        in_specs=[
-            pl.BlockSpec((2, PATCH, TILE), lambda i: (0, i, 0)),
-            pl.BlockSpec((2, 4, PATCH, PATCH), lambda i: (0, 0, i, 0)),
-            pl.BlockSpec((4, PATCH, PATCH), lambda i: (0, i, 0)),
-            pl.BlockSpec((2 * MODES, PATCH, PATCH), lambda i: (0, 0, 0)),
-            pl.BlockSpec((2, 4, PATCH, PATCH), lambda i: (0, 0, 0, 0)),
-            pl.BlockSpec((2, PATCH, PATCH), lambda i: (0, i, 0)),
-            pl.BlockSpec((2, PATCH, PATCH), lambda i: (0, 0, 0)),
+        in_specs=[ANY_SPEC] * 8,
+        out_specs=[ANY_SPEC] * 2,
+        input_output_aliases={0: 0},
+        scratch_shapes=[
+            pltpu.VMEM((2, PATCH, TILE), F32),
+            pltpu.VMEM((2, REST, PATCH), F32),
+            pltpu.VMEM((2, 4, PATCH, PATCH), F32),
+            pltpu.VMEM((2, REST, PATCH), F32),
+            pltpu.VMEM((4, PATCH, PATCH), F32),
+            pltpu.VMEM((REST, PATCH), F32),
+            pltpu.VMEM((2, 4, PATCH, PATCH), F32),
+            pltpu.VMEM((2, TILE, PATCH), F32),
+            pltpu.VMEM((2, PATCH, PATCH), F32),
+            pltpu.VMEM((2, PATCH, TILE), F32),
+            pltpu.VMEM((2, REST, PATCH), F32),
+            pltpu.VMEM((2 * MODES, PATCH, PATCH), F32),
+            pltpu.SemaphoreType.DMA((10,)),
+            pltpu.SemaphoreType.DMA((3,)),
         ],
-        out_specs=[
-            pl.BlockSpec((2, PATCH, TILE), lambda i: (0, i, 0)),
-            pl.BlockSpec((2 * MODES, PATCH, PATCH), lambda i: (0, 0, 0)),
-        ],
+        compiler_params=pltpu.CompilerParams(vmem_limit_bytes=56 * 2**20),
         name="finish",
-    )(obj, grad, weight, total, from_above, from_left, from_diag)
+    )(pre, obj, grad, weight, total, from_above, from_left, from_diag)
 
 
 def local(object_field, probe_modes, amplitude, positions, slot_counts):
@@ -748,13 +888,13 @@
     (right, lower, diag, *others), early, early_pg = halo_in(
         object_field, meta, probe_modes, tables, amp
     )
-    grad, weight, pg = patches(
+    pre, grad, weight, pg = patches(
         (meta, *others), probe_modes, tables, amp, early, early_pg,
         object_field, right, lower, diag,
     )
     total, from_above, from_left, from_diag = exchange(pg, grad)
     new_object, direction = finish(
-        object_field, grad, weight, total, from_above, from_left, from_diag
+        pre, object_field, grad, weight, total, from_above, from_left, from_diag
     )
     return new_object, direction.reshape(probe_modes.shape)
 

time: 96.1 us -> 89.9 us (0.935)
  Pallas kernels: 94.5 us -> 88.4 us
    pallas_call x1, Pallas kernels: 53.5 us -> 49.6 us  [exchange(): pl.pallas_call(exchange_kernel, out_shape=[jax.ShapeDtypeStruct((2 * MODE...]
    pallas_call x2, Pallas kernels: 13 us -> 10.4 us  [the longest x1 7.3 us: patches(): pl.pallas_call(patches_kernel, out_shape=[jax.ShapeDtypeStruct((2, TILE,...]
where the time goes in v5:
time: 89.9 us; the launch traced here: 89.7 us
  Pallas kernels  88.4 us (98%)
  between operations  1.31 us (1%)
    pallas_call x1, Pallas kernels, exchange(): pl.pallas_call(exchange_kernel, out_shape=[jax.ShapeDtypeStruct((2 * MODE...  49.6 us
    pallas_call x1, Pallas kernels, halo_in(): pl.pallas_call(halo_in_kernel, out_shape=[jax.ShapeDtypeStruct((2, TILE,...  26.6 us
    pallas_call x1, Pallas kernels, patches(): pl.pallas_call(patches_kernel, out_shape=[jax.ShapeDtypeStruct((2, TILE,...  7.3 us
    pallas_call x1, Pallas kernels, finish(): pl.pallas_call(finish_kernel, out_shape=[jax.ShapeDtypeStruct((2, TILE, T...  3.1 us

profile of v5, /device:TPU:1, one launch (start us, length us, event | category | flops | bytes accessed | tf_op | source)
XLA Modules:
  0.0 89.7 jit_solution(2797332244342173290)
XLA Ops:
  1.3 1.8 %plan.1.meta.meta_ref = s32[8,128]{1,0:T(8,128)} custom-call(s32[2,32]{1,0:T(2,128)} %bitcast.7, s32[1,1]{1,0:T(1,128)S(6)} %copy.11.count_ref), custom_call_target="tpu_custom_call" | custom-call | tf_op jit(solution)/shard_map/plan/pallas_call | solution.py:78
  3.1 26.6 %halo_in.1 = (f32[2,512,128]{2,1,0:T(8,128)}, f32[2,128,512]{2,1,0:T(8,128)}, f32[2,128,128]{2,1,0:T(8,128)}, s32[8,128]{1,0:T(8,128)}, s32[8,128]{1,0:T(8,128)}...) custom-call(f32[2,512,512]{2,1,0:T(8,128)} %obj.5, s32[8,128]{1,0:T(8,128)} %plan.1.meta.meta_ref, ...), custom_call_target="tpu_custom_call" | custom-call | tf_op jit(solution)/shard_map/halo_in/pallas_call | solution.py:350
  29.7 7.3 %patches.1 = (f32[2,512,512]{2,1,0:T(8,128)}, f32[2,5,640,128]{3,2,1,0:T(8,128)}, f32[4,512,128]{2,1,0:T(8,128)}, f32[9,128,128]{2,1,0:T(8,128)}) custom-call(s32[8,128]{1,0:T(8,128)} %plan.1.meta.meta_ref, s32[8,128]{1,0:T(8,128)} %get-tuple-element.20.meta_above, s32[8,128]{1,0:T(8,128)} %get-tuple-element.21.meta_left, ...), custom_call_target="tpu_custom_call" | custom-call | tf_op jit(solution)/shard_map/patches/pallas_call | solution.py:527
  37.0 49.6 %exchange.1 = (f32[8,128,128]{2,1,0:T(8,128)}, f32[2,4,128,128]{3,2,1,0:T(8,128)}, f32[2,512,128]{2,1,0:T(8,128)}, f32[2,128,128]{2,1,0:T(8,128)}) custom-call(f32[9,128,128]{2,1,0:T(8,128)} %get-tuple-element.31.pg_far, f32[2,5,640,128]{3,2,1,0:T(8,128)} %get-tuple-element.29.grad), custom_call_target="tpu_custom_call" | custom-call | tf_op jit(solution)/shard_map/exchange/pallas_call | solution.py:764
  86.6 3.1 %finish.1 = (f32[2,512,512]{2,1,0:T(8,128)}, f32[8,128,128]{2,1,0:T(8,128)}) custom-call(f32[2,512,512]{2,1,0:T(8,128)} %get-tuple-element.28.pre, f32[2,512,512]{2,1,0:T(8,128)} %obj.5, f32[2,5,640,128]{3,2,1,0:T(8,128)} %get-tuple-element.29.grad, f32[4,512,128]{2,1,0:T(8,128)} %get-tuple-element.30.weight, ...), custom_call_target="tpu_custom_call", output_to_operand_aliasing={{0}: (0, {})} | custom-call | tf_op jit(solution)/shard_map/finish/pallas_call | solution.py:852

commit v6 on v5

--- a/solution.py
+++ b/solution.py
@@ -485,18 +485,25 @@
     lt = lt_ref[...]
     rt = rt_ref[...]
 
-    def step(index, carry):
-        slots = []
-        for u in range(PAIR):
-            j = done + index * PAIR + u
-            slots.append((meta_ref[3, j], meta_ref[0, j], meta_ref[1, j], (j < count).astype(F32)))
-        grads = solve(slots, ext, 4, probe_ref, lt, rt, amp_ref, pg_ref)
-        for (s, row, at, live), (grad_re, grad_im) in zip(slots, grads):
-            scatter(grad_ref.at[0], row, at, grad_re)
-            scatter(grad_ref.at[1], row, at, grad_im)
-        return carry
-
-    lax.fori_loop(0, (count - done + PAIR - 1) // PAIR, step, 0)
+    def steps(first_slot, size, number):
+        def step(index, carry):
+            slots = []
+            for u in range(size):
+                j = first_slot + index * size + u
+                live = (j < count).astype(F32)
+                slots.append((meta_ref[3, j], meta_ref[0, j], meta_ref[1, j], live))
+            grads = solve(slots, ext, 4, probe_ref, lt, rt, amp_ref, pg_ref)
+            for (s, row, at, live), (grad_re, grad_im) in zip(slots, grads):
+                scatter(grad_ref.at[0], row, at, grad_re)
+                scatter(grad_ref.at[1], row, at, grad_im)
+            return carry
+
+        lax.fori_loop(0, number, step, 0)
+
+    whole = (count - done) // GROUP
+    left_over = done + whole * GROUP
+    steps(done, GROUP, whole)
+    steps(left_over, PAIR, (count - left_over + PAIR - 1) // PAIR)
     outward = [weights_out]
     low, top, between = pl.ds(TILE, PATCH), pl.ds(0, PATCH), pl.ds(PATCH, REST)
     for source, dest in (
@@ -593,13 +600,12 @@
 
     load = pltpu.make_async_copy(pg_far, pg, loaded)
     load.start()
-    load.wait()
     pl.semaphore_wait(barrier, 17 + jnp.where(relays, 1, 0))
 
     zeroth = []
     for d in range(1, 9):
         p = lax.rem(chip + d, 8)
-        copy = remote(pg.at[:, rows(p, 1 - core), :], buf0.at[d - 1], s0.at[d - 1], r0.at[d - 1], sibling)
+        copy = remote(pg_far.at[:, rows(p, 1 - core), :], buf0.at[d - 1], s0.at[d - 1], r0.at[d - 1], sibling)
         copy.start()
         zeroth.append(copy)
 
@@ -651,7 +657,8 @@
             for r in reversed(range(ROUTES)):
                 to_relay(r, j).start()
 
-    post_rows(DIRECT, 40, near_send, near_get)
+    post_rows(DIRECT, 16, near_send, near_get)
+    load.wait()
     first = []
     for d in range(1, 8):
         p = lax.rem(chip + d, 8)
@@ -663,7 +670,7 @@
     zeroth[7].wait_recv()
     acc = pg[:, rows(chip, core), :] + buf0[7]
 
-    post_rows(DIRECT + 40, 40, near_send, near_get)
+    post_rows(DIRECT + 16, 32, near_send, near_get)
     post(
         grad.at[:, 4, pl.ds(TILE, PATCH), :], from_diag, (below, after),
         downs & rights, ups & lefts,
@@ -682,8 +689,6 @@
         copy.start()
         second.append(copy)
     pass_on(range(2, CHUNKS))
-    post_rows(0, DIRECT, downs, ups)
-    post_rows(DIRECT + 80, 40, near_send, near_get)
     post_columns(0, 256)
     acc = red1[planes(y)]
     for d in range(1, 4):
@@ -721,6 +726,8 @@
     copy.start()
     sixth.append(copy)
     total[:, mine, :] = res[...]
+    post_rows(DIRECT + 48, 72, near_send, near_get)
+    post_rows(0, DIRECT, downs, ups)
     for d in range(1, 8):
         at = rows(lax.rem(chip + 8 - d, 8), core)
         remote(res, total.at[:, at, :], s5.at[d], r5.at[d], chips[d - 1]).wait_recv()

time: 89.9 us -> 85.4 us (0.950)
  Pallas kernels: 88.4 us -> 83.8 us
    pallas_call x1, Pallas kernels: 49.6 us -> 46.4 us  [exchange(): pl.pallas_call(exchange_kernel, out_shape=[jax.ShapeDtypeStruct((2 * MODE...]
    pallas_call x1, Pallas kernels: 7.3 us -> 5.93 us  [patches(): pl.pallas_call(patches_kernel, out_shape=[jax.ShapeDtypeStruct((2, TILE,...]
where the time goes in v6:
time: 85.4 us; the launch traced here: 85.1 us
  Pallas kernels  83.8 us (98%)
  between operations  1.31 us (2%)
    pallas_call x1, Pallas kernels, exchange(): pl.pallas_call(exchange_kernel, out_shape=[jax.ShapeDtypeStruct((2 * MODE...  46.4 us
    pallas_call x1, Pallas kernels, halo_in(): pl.pallas_call(halo_in_kernel, out_shape=[jax.ShapeDtypeStruct((2, TILE,...  26.6 us
    pallas_call x1, Pallas kernels, patches(): pl.pallas_call(patches_kernel, out_shape=[jax.ShapeDtypeStruct((2, TILE,...  5.93 us
    pallas_call x1, Pallas kernels, finish(): pl.pallas_call(finish_kernel, out_shape=[jax.ShapeDtypeStruct((2, TILE, T...  3.1 us
    pallas_call x1, Pallas kernels, plan(): pl.pallas_call(plan_kernel, out_shape=jax.ShapeDtypeStruct((8, PATCH), jn...  1.79 us

profile of v6, /device:TPU:1, one launch (start us, length us, event | category | flops | bytes accessed | tf_op | source)
XLA Modules:
  0.0 85.1 jit_solution(17148856429297548833)
XLA Ops:
  1.3 1.8 %plan.1.meta.meta_ref = s32[8,128]{1,0:T(8,128)} custom-call(s32[2,32]{1,0:T(2,128)} %bitcast.7, s32[1,1]{1,0:T(1,128)S(6)} %copy.11.count_ref), custom_call_target="tpu_custom_call" | custom-call | tf_op jit(solution)/shard_map/plan/pallas_call | solution.py:78
  3.1 26.6 %halo_in.1 = (f32[2,512,128]{2,1,0:T(8,128)}, f32[2,128,512]{2,1,0:T(8,128)}, f32[2,128,128]{2,1,0:T(8,128)}, s32[8,128]{1,0:T(8,128)}, s32[8,128]{1,0:T(8,128)}...) custom-call(f32[2,512,512]{2,1,0:T(8,128)} %obj.5, s32[8,128]{1,0:T(8,128)} %plan.1.meta.meta_ref, ...), custom_call_target="tpu_custom_call" | custom-call | tf_op jit(solution)/shard_map/halo_in/pallas_call | solution.py:350
  29.7 5.9 %patches.1 = (f32[2,512,512]{2,1,0:T(8,128)}, f32[2,5,640,128]{3,2,1,0:T(8,128)}, f32[4,512,128]{2,1,0:T(8,128)}, f32[9,128,128]{2,1,0:T(8,128)}) custom-call(s32[8,128]{1,0:T(8,128)} %plan.1.meta.meta_ref, s32[8,128]{1,0:T(8,128)} %get-tuple-element.20.meta_above, s32[8,128]{1,0:T(8,128)} %get-tuple-element.21.meta_left, ...), custom_call_target="tpu_custom_call" | custom-call | tf_op jit(solution)/shard_map/patches/pallas_call | solution.py:534
  35.6 46.4 %exchange.1 = (f32[8,128,128]{2,1,0:T(8,128)}, f32[2,4,128,128]{3,2,1,0:T(8,128)}, f32[2,512,128]{2,1,0:T(8,128)}, f32[2,128,128]{2,1,0:T(8,128)}) custom-call(f32[9,128,128]{2,1,0:T(8,128)} %get-tuple-element.31.pg_far, f32[2,5,640,128]{3,2,1,0:T(8,128)} %get-tuple-element.29.grad), custom_call_target="tpu_custom_call" | custom-call | tf_op jit(solution)/shard_map/exchange/pallas_call | solution.py:771
  82.0 3.1 %finish.1 = (f32[2,512,512]{2,1,0:T(8,128)}, f32[8,128,128]{2,1,0:T(8,128)}) custom-call(f32[2,512,512]{2,1,0:T(8,128)} %get-tuple-element.28.pre, f32[2,512,512]{2,1,0:T(8,128)} %obj.5, f32[2,5,640,128]{3,2,1,0:T(8,128)} %get-tuple-element.29.grad, f32[4,512,128]{2,1,0:T(8,128)} %get-tuple-element.30.weight, ...), custom_call_target="tpu_custom_call", output_to_operand_aliasing={{0}: (0, {})} | custom-call | tf_op jit(solution)/shard_map/finish/pallas_call | solution.py:859

commit v7 on v6

--- a/solution.py
+++ b/solution.py
@@ -67,8 +67,7 @@
         middle = middle + jnp.where(outer, 1, 0)
         high = high + jnp.where(live & jnp.logical_not(upper), 1, 0)
     for line in (0, 1, 3):
-        for past in range(pos_ref.shape[1], pos_ref.shape[1] + EARLY):
-            meta_ref[line, past] = 0
+        meta_ref[line, pos_ref.shape[1]] = 0
     meta_ref[2, 0] = count
     meta_ref[2, 1] = inner_count
     meta_ref[2, 2] = upper_count
@@ -291,8 +290,8 @@
         put(index).start()
 
         for half in range(2):
-            @pl.when(relays & (index > 0) & (2 * index + half < CHUNKS + 2))
-            def _(j=2 * index + half - 2):
+            @pl.when(relays & (2 * index + half < CHUNKS))
+            def _(j=2 * index + half):
                 to_relay(0, j).wait_recv()
                 onward(route, j).start()
 
@@ -444,33 +443,37 @@
     ):
         live_there = ref[2, 0] if there is None else jnp.where(there, ref[2, 0], 0)
 
-        def weigh(s, carry, ref=ref, down=down, side=side):
-            row, at = ref[0, s] + (PATCH - down), ref[1, s] + (PATCH - side)
-            touches = None
-            if down:
-                touches = row > 0
-            if side:
-                touches = at > 0 if touches is None else touches & (at > 0)
-            if touches is None:
-                scatter(spread, row, at, power)
-            else:
-                pl.when(touches)(lambda: scatter(spread, row, at, power))
+        def weigh(index, carry, ref=ref, down=down, side=side, live_there=live_there):
+            for s in (2 * index, 2 * index + 1):
+                row, at = ref[0, s] + (PATCH - down), ref[1, s] + (PATCH - side)
+                live = s < live_there
+                if down or side:
+                    touches = live
+                    if down:
+                        touches = touches & (row > 0)
+                    if side:
+                        touches = touches & (at > 0)
+                    pl.when(touches)(functools.partial(scatter, spread, row, at, power))
+                else:
+                    scatter(spread, row, at, power * live.astype(F32))
             return carry
 
-        lax.fori_loop(0, live_there, weigh, 0)
+        lax.fori_loop(0, (live_there + 1) // 2, weigh, 0)
     weights_out = pltpu.make_async_copy(
         spread.at[pl.ds(1, 4), pl.ds(PATCH, TILE), :], weight, stored.at[0]
     )
     weights_out.start()
     copies[at_first].wait()
 
-    def place(j, carry):
-        held = jnp.where(j < base, j, j - base + FIRST)
-        for p in range(2):
-            scatter(grad_ref.at[p], meta_ref[0, j], meta_ref[1, j], early_ref[held, p])
+    def place(index, carry):
+        for j in (2 * index, 2 * index + 1):
+            held = jnp.minimum(jnp.where(j < base, j, j - base + FIRST), EARLY - 1)
+            for p in range(2):
+                value = jnp.where(j < done, early_ref[held, p], 0.0)
+                scatter(grad_ref.at[p], meta_ref[0, j], meta_ref[1, j], value)
         return carry
 
-    lax.fori_loop(0, done, place, 0)
+    lax.fori_loop(0, (done + 1) // 2, place, 0)
     for copy in copies[at_first + 1 :]:
         copy.wait()
 

time: 85.4 us -> 83.4 us (0.977); the launches traced: 85.1 us -> 84.1 us
  Pallas kernels: 83.8 us -> 82.8 us
    pallas_call x1, Pallas kernels: 46.4 us -> 45.3 us  [exchange(): pl.pallas_call(exchange_kernel, out_shape=[jax.ShapeDtypeStruct((2 * MODE...]
where the time goes in v7:
time: 83.4 us; the launch traced here: 84.1 us
  Pallas kernels  82.8 us (99%)
  between operations  1.31 us (2%)
    pallas_call x1, Pallas kernels, exchange(): pl.pallas_call(exchange_kernel, out_shape=[jax.ShapeDtypeStruct((2 * MODE...  45.3 us
    pallas_call x1, Pallas kernels, halo_in(): pl.pallas_call(halo_in_kernel, out_shape=[jax.ShapeDtypeStruct((2, TILE,...  26.6 us
    pallas_call x1, Pallas kernels, patches(): pl.pallas_call(patches_kernel, out_shape=[jax.ShapeDtypeStruct((2, TILE,...  6.05 us
    pallas_call x1, Pallas kernels, finish(): pl.pallas_call(finish_kernel, out_shape=[jax.ShapeDtypeStruct((2, TILE, T...  3.1 us
    pallas_call x1, Pallas kernels, plan(): pl.pallas_call(plan_kernel, out_shape=jax.ShapeDtypeStruct((8, PATCH), jn...  1.76 us

profile of v7, /device:TPU:1, one launch (start us, length us, event | category | flops | bytes accessed | tf_op | source)
XLA Modules:
  0.0 84.1 jit_solution(3349357763085421773)
XLA Ops:
  1.3 1.8 %plan.1.meta.meta_ref = s32[8,128]{1,0:T(8,128)} custom-call(s32[2,32]{1,0:T(2,128)} %bitcast.7, s32[1,1]{1,0:T(1,128)S(6)} %copy.11.count_ref), custom_call_target="tpu_custom_call" | custom-call | tf_op jit(solution)/shard_map/plan/pallas_call | solution.py:77
  3.0 26.6 %halo_in.1 = (f32[2,512,128]{2,1,0:T(8,128)}, f32[2,128,512]{2,1,0:T(8,128)}, f32[2,128,128]{2,1,0:T(8,128)}, s32[8,128]{1,0:T(8,128)}, s32[8,128]{1,0:T(8,128)}...) custom-call(f32[2,512,512]{2,1,0:T(8,128)} %obj.5, s32[8,128]{1,0:T(8,128)} %plan.1.meta.meta_ref, ...), custom_call_target="tpu_custom_call" | custom-call | tf_op jit(solution)/shard_map/halo_in/pallas_call | solution.py:349
  29.6 6.0 %patches.1 = (f32[2,512,512]{2,1,0:T(8,128)}, f32[2,5,640,128]{3,2,1,0:T(8,128)}, f32[4,512,128]{2,1,0:T(8,128)}, f32[9,128,128]{2,1,0:T(8,128)}) custom-call(s32[8,128]{1,0:T(8,128)} %plan.1.meta.meta_ref, s32[8,128]{1,0:T(8,128)} %get-tuple-element.20.meta_above, s32[8,128]{1,0:T(8,128)} %get-tuple-element.21.meta_left, ...), custom_call_target="tpu_custom_call" | custom-call | tf_op jit(solution)/shard_map/patches/pallas_call | solution.py:537
  35.7 45.3 %exchange.1 = (f32[8,128,128]{2,1,0:T(8,128)}, f32[2,4,128,128]{3,2,1,0:T(8,128)}, f32[2,512,128]{2,1,0:T(8,128)}, f32[2,128,128]{2,1,0:T(8,128)}) custom-call(f32[9,128,128]{2,1,0:T(8,128)} %get-tuple-element.31.pg_far, f32[2,5,640,128]{3,2,1,0:T(8,128)} %get-tuple-element.29.grad), custom_call_target="tpu_custom_call" | custom-call | tf_op jit(solution)/shard_map/exchange/pallas_call | solution.py:774
  81.0 3.1 %finish.1 = (f32[2,512,512]{2,1,0:T(8,128)}, f32[8,128,128]{2,1,0:T(8,128)}) custom-call(f32[2,512,512]{2,1,0:T(8,128)} %get-tuple-element.28.pre, f32[2,512,512]{2,1,0:T(8,128)} %obj.5, f32[2,5,640,128]{3,2,1,0:T(8,128)} %get-tuple-element.29.grad, f32[4,512,128]{2,1,0:T(8,128)} %get-tuple-element.30.weight, ...), custom_call_target="tpu_custom_call", output_to_operand_aliasing={{0}: (0, {})} | custom-call | tf_op jit(solution)/shard_map/finish/pallas_call | solution.py:862

commit v8 on v7

--- a/solution.py
+++ b/solution.py
@@ -444,7 +444,7 @@
         live_there = ref[2, 0] if there is None else jnp.where(there, ref[2, 0], 0)
 
         def weigh(index, carry, ref=ref, down=down, side=side, live_there=live_there):
-            for s in (2 * index, 2 * index + 1):
+            for s in [4 * index + u for u in range(4)]:
                 row, at = ref[0, s] + (PATCH - down), ref[1, s] + (PATCH - side)
                 live = s < live_there
                 if down or side:
@@ -458,7 +458,7 @@
                     scatter(spread, row, at, power * live.astype(F32))
             return carry
 
-        lax.fori_loop(0, (live_there + 1) // 2, weigh, 0)
+        lax.fori_loop(0, (live_there + 3) // 4, weigh, 0)
     weights_out = pltpu.make_async_copy(
         spread.at[pl.ds(1, 4), pl.ds(PATCH, TILE), :], weight, stored.at[0]
     )
@@ -466,14 +466,14 @@
     copies[at_first].wait()
 
     def place(index, carry):
-        for j in (2 * index, 2 * index + 1):
+        for j in [4 * index + u for u in range(4)]:
             held = jnp.minimum(jnp.where(j < base, j, j - base + FIRST), EARLY - 1)
             for p in range(2):
                 value = jnp.where(j < done, early_ref[held, p], 0.0)
                 scatter(grad_ref.at[p], meta_ref[0, j], meta_ref[1, j], value)
         return carry
 
-    lax.fori_loop(0, (done + 1) // 2, place, 0)
+    lax.fori_loop(0, (done + 3) // 4, place, 0)
     for copy in copies[at_first + 1 :]:
         copy.wait()
 

time: 83.4 us -> 83.6 us (level); the launches traced: 84.1 us -> 82.9 us
  Pallas kernels: 82.8 us -> 81.6 us
    pallas_call x1, Pallas kernels: 45.3 us -> 41.3 us  [exchange(): pl.pallas_call(exchange_kernel, out_shape=[jax.ShapeDtypeStruct((2 * MODE...]
    pallas_call x1, Pallas kernels: 6.05 us -> 8.89 us  [patches(): pl.pallas_call(patches_kernel, out_shape=[jax.ShapeDtypeStruct((2, TILE,...]
where the time goes in v8:
time: 83.6 us; the launch traced here: 82.9 us
  Pallas kernels  81.6 us (98%)
  between operations  1.31 us (2%)
    pallas_call x1, Pallas kernels, exchange(): pl.pallas_call(exchange_kernel, out_shape=[jax.ShapeDtypeStruct((2 * MODE...  41.3 us
    pallas_call x1, Pallas kernels, halo_in(): pl.pallas_call(halo_in_kernel, out_shape=[jax.ShapeDtypeStruct((2, TILE,...  26.6 us
    pallas_call x1, Pallas kernels, patches(): pl.pallas_call(patches_kernel, out_shape=[jax.ShapeDtypeStruct((2, TILE,...  8.89 us
    pallas_call x1, Pallas kernels, finish(): pl.pallas_call(finish_kernel, out_shape=[jax.ShapeDtypeStruct((2, TILE, T...  3.1 us
    pallas_call x1, Pallas kernels, plan(): pl.pallas_call(plan_kernel, out_shape=jax.ShapeDtypeStruct((8, PATCH), jn...  1.76 us

profile of v8, /device:TPU:1, one launch (start us, length us, event | category | flops | bytes accessed | tf_op | source)
XLA Modules:
  0.0 82.9 jit_solution(12527745459272162081)
XLA Ops:
  1.3 1.8 %plan.1.meta.meta_ref = s32[8,128]{1,0:T(8,128)} custom-call(s32[2,32]{1,0:T(2,128)} %bitcast.7, s32[1,1]{1,0:T(1,128)S(6)} %copy.11.count_ref), custom_call_target="tpu_custom_call" | custom-call | tf_op jit(solution)/shard_map/plan/pallas_call | solution.py:77
  3.0 26.6 %halo_in.1 = (f32[2,512,128]{2,1,0:T(8,128)}, f32[2,128,512]{2,1,0:T(8,128)}, f32[2,128,128]{2,1,0:T(8,128)}, s32[8,128]{1,0:T(8,128)}, s32[8,128]{1,0:T(8,128)}...) custom-call(f32[2,512,512]{2,1,0:T(8,128)} %obj.5, s32[8,128]{1,0:T(8,128)} %plan.1.meta.meta_ref, ...), custom_call_target="tpu_custom_call" | custom-call | tf_op jit(solution)/shard_map/halo_in/pallas_call | solution.py:349
  29.6 8.9 %patches.1 = (f32[2,512,512]{2,1,0:T(8,128)}, f32[2,5,640,128]{3,2,1,0:T(8,128)}, f32[4,512,128]{2,1,0:T(8,128)}, f32[9,128,128]{2,1,0:T(8,128)}) custom-call(s32[8,128]{1,0:T(8,128)} %plan.1.meta.meta_ref, s32[8,128]{1,0:T(8,128)} %get-tuple-element.20.meta_above, s32[8,128]{1,0:T(8,128)} %get-tuple-element.21.meta_left, ...), custom_call_target="tpu_custom_call" | custom-call | tf_op jit(solution)/shard_map/patches/pallas_call | solution.py:537
  38.5 41.3 %exchange.1 = (f32[8,128,128]{2,1,0:T(8,128)}, f32[2,4,128,128]{3,2,1,0:T(8,128)}, f32[2,512,128]{2,1,0:T(8,128)}, f32[2,128,128]{2,1,0:T(8,128)}) custom-call(f32[9,128,128]{2,1,0:T(8,128)} %get-tuple-element.31.pg_far, f32[2,5,640,128]{3,2,1,0:T(8,128)} %get-tuple-element.29.grad), custom_call_target="tpu_custom_call" | custom-call | tf_op jit(solution)/shard_map/exchange/pallas_call | solution.py:774
  79.8 3.1 %finish.1 = (f32[2,512,512]{2,1,0:T(8,128)}, f32[8,128,128]{2,1,0:T(8,128)}) custom-call(f32[2,512,512]{2,1,0:T(8,128)} %get-tuple-element.28.pre, f32[2,512,512]{2,1,0:T(8,128)} %obj.5, f32[2,5,640,128]{3,2,1,0:T(8,128)} %get-tuple-element.29.grad, f32[4,512,128]{2,1,0:T(8,128)} %get-tuple-element.30.weight, ...), custom_call_target="tpu_custom_call", output_to_operand_aliasing={{0}: (0, {})} | custom-call | tf_op jit(solution)/shard_map/finish/pallas_call | solution.py:862
